TPU v7x, 32 devices: a whole 2x2x4 slice. The times are simulated.
32 devices in a mesh: section: 4 (over y, x), seq: 8 (over z, core).
Axes of the slice: x: 2, y: 2, z: 4, core: 2. Of those that a mesh axis runs over, the one named last changes fastest.
Arguments:
- latents: bfloat16 [2, 320, 1536], P(None, 'seq'), may hold values from -6 to 6
- lengths: int32 [2], replicated, may hold values from 1 to 320, as said below
- segment_layers: int32 [4], P('section'), may hold values from 1 to 2, as said below
- norm_gain: bfloat16 [8, 1536], P('section'), may hold values from 0.3984375 to 1.59375
- qkv_weight: bfloat16 [8, 1536, 2304], P('section'), may hold values from -0.15625 to 0.15625
- qk_gain: bfloat16 [8, 128], P('section'), may hold values from 0.25 to 1.75
- out_weight: bfloat16 [8, 768, 1536], P('section'), may hold values from -0.21875 to 0.21875
Outputs:
- denoised: bfloat16 [2, 320, 1536], P(None, 'seq', 'section')
Inputs may be any that keep to these rules, and one draw needn't show every extreme that they name: `lengths`: one micro-batch in every draw has all 320 tokens live. `segment_layers`: some section runs all 2 slots and some section runs one.
All inputs are finite; a program needn't handle non-finite values.
Results may differ from a plain program's by a relative error of at most 0.023.
Values may be sent and summed in bfloat16 or wider, within the bound.
No kernel may reach another device: no remote copies, remote signals or barrier semaphores. Data moves between devices by JAX's collectives and lax.ppermute only.
A program may use at most 128 MiB of HBM per device.

v0:
```python
import functools

import jax
import jax.numpy as jnp
from jax import lax
from jax.experimental import pallas as pl
from jax.experimental.pallas import tpu as pltpu
from jax.sharding import PartitionSpec as P

eps_norm = 1e-06
neg_large = -1e30
F32, BF16 = jnp.float32, jnp.bfloat16
TILE = 256


def shifted(value, axis, steps):
    count = lax.axis_size(axis)
    leading, last = (max(0, -steps), min(count, count - steps))
    return lax.ppermute(value, axis, [(source, source + steps) for source in range(leading, last)])


def rms_scale(values, gain_vec):
    return (
        values * lax.rsqrt(jnp.mean(values * values, axis=-1, keepdims=True) + eps_norm) * gain_vec
    )


def body_layer(current, length, norm_w, qkv_w, qk_w, out_w):
    tok_rows, width = current.shape
    inner = qkv_w.shape[1] // 3
    head_dim = qk_w.shape[0] // 2
    head_count = inner // head_dim
    resid = current.astype(jnp.float32)
    normed = rms_scale(resid, norm_w.astype(jnp.float32)).astype(jnp.bfloat16)
    projected = jnp.dot(normed, qkv_w, preferred_element_type=jnp.float32)
    queries = rms_scale(
        projected[:, :inner].reshape(tok_rows, head_count, head_dim),
        qk_w[:head_dim].astype(jnp.float32),
    ).astype(jnp.bfloat16)
    keys = (
        rms_scale(
            projected[:, inner : 2 * inner].reshape(tok_rows, head_count, head_dim),
            qk_w[head_dim:].astype(jnp.float32),
        )
        .astype(jnp.bfloat16)
        .reshape(tok_rows, inner)
    )
    values = projected[:, 2 * inner :].astype(jnp.bfloat16)
    score_scale = head_dim ** (-0.5)
    run_max = jnp.full((head_count, tok_rows), neg_large, jnp.float32)
    key_block = lax.all_gather(keys, "seq", axis=0, tiled=True)
    value_block = lax.all_gather(values, "seq", axis=0, tiled=True)
    block_rows = key_block.shape[0]
    key_heads = key_block.reshape(block_rows, head_count, head_dim)
    value_heads = value_block.reshape(block_rows, head_count, head_dim)
    scores = (
        jnp.einsum("qhd,khd->hqk", queries, key_heads, preferred_element_type=jnp.float32)
        * score_scale
    )
    positions = jnp.arange(block_rows, dtype=jnp.int32)
    scores = jnp.where((positions < length)[None, None, :], scores, neg_large)
    new_max = jnp.maximum(run_max, jnp.max(scores, axis=-1))
    weights = jnp.exp(scores - new_max[..., None])
    run_total = jnp.sum(weights, axis=-1)
    run_acc = jnp.einsum(
        "hqk,khd->hqd",
        weights.astype(jnp.bfloat16),
        value_heads,
        preferred_element_type=jnp.float32,
    )
    run_max, run_total, run_acc = (new_max, run_total, run_acc)
    attended = (run_acc / run_total[..., None]).astype(jnp.bfloat16)
    update = jnp.einsum(
        "hqd,hde->qe",
        attended,
        out_w.reshape(head_count, head_dim, width),
        preferred_element_type=jnp.float32,
    )
    return (resid + update).astype(jnp.bfloat16)


def relay_local(latents, lengths, segment_layers, norm_gain, qkv_weight, qk_gain, out_weight):
    segment_count = lax.axis_size("section")
    segment_pos = lax.axis_index("section")
    micro_count, tok_rows, width = latents.shape
    slot_count = qkv_weight.shape[0]
    own_layers = segment_layers[0]
    tick_count = micro_count + segment_count - 1

    def slot_layer(slot_index, current, length):
        return body_layer(
            current,
            length,
            lax.dynamic_index_in_dim(norm_gain, slot_index, 0, False),
            lax.dynamic_index_in_dim(qkv_weight, slot_index, 0, False),
            lax.dynamic_index_in_dim(qk_gain, slot_index, 0, False),
            lax.dynamic_index_in_dim(out_weight, slot_index, 0, False),
        )

    def advance(tick_index, loop_state):
        received, finished = loop_state
        micro_index = tick_index - segment_pos
        is_valid = (micro_index >= 0) & (micro_index < micro_count)
        clipped = jnp.clip(micro_index, 0, micro_count - 1)
        entering = lax.dynamic_index_in_dim(latents, clipped, 0, False)
        current = jnp.where(segment_pos == 0, entering, received)
        length = lax.dynamic_index_in_dim(lengths, clipped, 0, False)
        for slot_index in range(slot_count):
            updated = slot_layer(slot_index, current, length)
            current = jnp.where(slot_index < own_layers, updated, current)
        previous = lax.dynamic_index_in_dim(finished, clipped, 0, True)
        keep_it = is_valid & (segment_pos == segment_count - 1)
        finished = lax.dynamic_update_index_in_dim(
            finished, jnp.where(keep_it, current[None], previous), clipped, 0
        )
        received = shifted(current, "section", 1)
        return (received, finished)

    start_state = (
        jnp.zeros((tok_rows, width), jnp.bfloat16),
        jnp.zeros((micro_count, tok_rows, width), jnp.bfloat16),
    )
    final_state = lax.fori_loop(0, tick_count, advance, start_state)
    finished = final_state[1]
    terms = jnp.where(segment_pos == segment_count - 1, finished.astype(jnp.float32), 0.0)
    return lax.psum_scatter(terms.astype(jnp.bfloat16), "section", scatter_dimension=2, tiled=True)


LOG2E = 1.4426950408889634


def row_of(ref, slot, first=0, slots=2):
    row = ref[first : first + 1, :]
    for n in range(1, slots):
        row = jnp.where(slot == n, ref[first + n : first + n + 1, :], row)
    return row


def norm_rows(dst, src, start, gain):
    for row in range(0, dst.shape[0], 16):
        values = src[pl.ds(start + row, 16), :].astype(F32)
        mean = jnp.mean(values * values, axis=-1, keepdims=True)
        dst[row : row + 16, :] = (values * lax.rsqrt(mean + eps_norm) * gain).astype(BF16)


def head_norm(acc, gain, head_ones):
    mean = jnp.dot((acc * acc).astype(BF16), head_ones[...], preferred_element_type=F32)
    return (acc * lax.rsqrt(mean + eps_norm) * gain).astype(BF16)


def spread_heads(dst, tile, block, start, head_dim):
    per_tile = TILE // head_dim
    rows = dst.shape[1] // per_tile
    lane = lax.broadcasted_iota(jnp.int32, (1, TILE), 1) // head_dim
    for h in range(per_tile):
        dst[tile, pl.ds(h * rows + start, block.shape[0]), :] = jnp.where(lane == h, block, jnp.zeros_like(block))


def head_totals(weights, rows, head_dim):
    half = lax.broadcasted_iota(jnp.int32, (1, 128), 1) < 64
    totals = []
    for h in range(TILE // head_dim):
        low, high = h * rows, (h + 1) * rows
        total = None
        for at in range(low // 128 * 128, high, 128):
            piece = weights[:, at : at + 128]
            if at < low:
                piece = jnp.where(half, 0.0, piece)
            elif at + 128 > high:
                piece = jnp.where(half, piece, 0.0)
            total = piece if total is None else total + piece
        totals.append(1.0 / jnp.sum(total, axis=-1, keepdims=True))
    return totals


def keep_kernel(head_dim, lengths, qkv_hbm, norm_gain, qk_gain, qkv_w, norm_g, gains, bias, head_ones, token, sem):
    copy = pltpu.make_async_copy(qkv_hbm, qkv_w, sem)
    copy.start()
    slots = norm_gain.shape[0]
    per_tile = TILE // head_dim
    norm_g[...] = norm_gain[...].astype(F32)
    rows_gain = qk_gain[...].astype(F32)
    both = [jnp.concatenate([rows_gain[:, n * head_dim : (n + 1) * head_dim]] * per_tile, axis=1) for n in range(2)]
    gains[...] = jnp.concatenate(both, axis=0)
    lane_head = lax.broadcasted_iota(jnp.int32, (TILE, TILE), 1) // head_dim
    row_head = lax.broadcasted_iota(jnp.int32, (TILE, TILE), 0) // head_dim
    head_ones[...] = jnp.where(lane_head == row_head, 1.0 / head_dim, 0.0).astype(BF16)
    chips = lax.axis_size("seq") // 2
    seq = lax.axis_index("seq")
    chip, core = seq // 2, seq % 2
    rows = bias.shape[1] // per_tile
    piece = rows // chips // 2
    row = lax.broadcasted_iota(jnp.int32, (1, bias.shape[1]), 1) % rows
    number, half = row // piece % chips, row // (piece * chips)
    owner = half ^ core
    order = row // piece % chips
    micro = chip // (chips // lengths.shape[0])
    later = 2 * (owner ^ micro) + order // 2, owner ^ ((order + order // 2) % 2)
    length = lengths[micro]
    biases = []
    for block, from_core in ((number, owner), later):
        live = piece * (2 * (block ^ chip) + from_core) + row % piece < length
        for slot in range(slots):
            most = jnp.max(jnp.abs(both[0][slot : slot + 1])) * jnp.max(jnp.abs(both[1][slot : slot + 1]))
            biases.append(jnp.where(live, -1.01 * head_dim**0.5 * LOG2E * most, neg_large))
    bias[...] = jnp.concatenate(biases, axis=0)
    token[...] = jnp.zeros_like(token)
    copy.wait()


def keep_out_kernel(after, out_hbm, out_w, sem):
    copy = pltpu.make_async_copy(out_hbm, out_w, sem)
    copy.start()
    copy.wait()


def keep_out(after, out_w):
    far = pl.BlockSpec(memory_space=pltpu.HBM)
    whole = pl.BlockSpec(memory_space=pltpu.VMEM)
    return pl.pallas_call(
        keep_out_kernel,
        out_shape=pltpu.VMEM(out_w.shape, BF16),
        in_specs=[whole, far],
        out_specs=whole,
        scratch_shapes=[pltpu.SemaphoreType.DMA],
        compiler_params=pltpu.CompilerParams(vmem_limit_bytes=28 * 2**20),
        cost_estimate=pl.CostEstimate(flops=0, bytes_accessed=4 * out_w.size, transcendentals=0),
        name="keep_out",
    )(after, out_w)


def keep_weights(lengths, qkv_w, norm_gain, qk_gain, rows):
    far = pl.BlockSpec(memory_space=pltpu.HBM)
    whole = pl.BlockSpec(memory_space=pltpu.VMEM)
    small = pl.BlockSpec(memory_space=pltpu.SMEM)
    head_dim, slots = qk_gain.shape[1] // 2, qk_gain.shape[0]
    return pl.pallas_call(
        functools.partial(keep_kernel, head_dim),
        out_shape=[
            pltpu.VMEM(qkv_w.shape, BF16),
            pltpu.VMEM(norm_gain.shape, F32),
            pltpu.VMEM((2 * slots, TILE), F32),
            pltpu.VMEM((2 * slots, TILE // head_dim * rows), F32),
            pltpu.VMEM((TILE, TILE), BF16),
            pltpu.VMEM((8, 128), F32),
        ],
        in_specs=[small, far, whole, whole],
        out_specs=[whole] * 6,
        scratch_shapes=[pltpu.SemaphoreType.DMA],
        compiler_params=pltpu.CompilerParams(vmem_limit_bytes=40 * 2**20),
        cost_estimate=pl.CostEstimate(flops=0, bytes_accessed=4 * qkv_w.size, transcendentals=0),
        name="keep_weights",
    )(lengths, qkv_w, norm_gain, qk_gain)


def join_kernel(token, *refs):
    pieces, out = refs[:-1], refs[-1]
    out[...] = jnp.concatenate([piece[...].astype(F32) for piece in pieces], axis=0).astype(BF16)


def join_pieces(token, pieces):
    token = pltpu.with_memory_space_constraint(token, pltpu.VMEM)
    whole = pl.BlockSpec(memory_space=pltpu.VMEM)
    return pl.pallas_call(
        join_kernel,
        out_shape=jax.ShapeDtypeStruct((sum(piece.shape[0] for piece in pieces), pieces[0].shape[1]), BF16),
        in_specs=[whole] * (1 + len(pieces)),
        out_specs=whole,
        compiler_params=pltpu.CompilerParams(vmem_limit_bytes=8 * 2**20),
        name="join_pieces",
    )(token, *pieces)


def project_half(src, src_start, start, slot, head_dim, xn, k_s, v_s, q_s, qkv_w, norm_g, gains, head_ones):
    slots, inner = qkv_w.shape[0], qkv_w.shape[2] // 3
    tiles = inner // TILE
    q_gain, k_gain = row_of(gains, slot, 0, slots), row_of(gains, slot, slots, slots)
    norm_rows(xn, src, src_start, row_of(norm_g, slot, 0, slots))

    def keep(kind, t, acc):
        if kind == 0:
            q_s[pl.ds(start, acc.shape[0]), t * TILE : (t + 1) * TILE] = head_norm(acc, q_gain, head_ones)
        elif kind == 1:
            spread_heads(k_s, t, head_norm(acc, k_gain, head_ones), start, head_dim)
        else:
            spread_heads(v_s, t, acc.astype(BF16), start, head_dim)

    waiting = None
    for kind, t in [(kind, t) for kind in (1, 0, 2) for t in range(tiles)]:
        at = kind * inner + t * TILE
        acc = jnp.dot(xn[...], qkv_w[slot, :, at : at + TILE], preferred_element_type=F32)
        if waiting is not None:
            keep(*waiting)
        waiting = (kind, t, acc)
    keep(*waiting)


def attend_rows(starts, part, key_bias, slot, head_dim, x_s, att, k_s, v_s, q_s, out_w):
    rows = x_s.shape[0]
    inner, width = out_w.shape[1:]
    parts = [pl.ds(pl.multiple_of(start, 16), part) for start in starts]
    half = lax.broadcasted_iota(jnp.int32, (1, 128), 1) < 64
    for t in range(inner // TILE):
        queries = jnp.concatenate([q_s[rows_of, t * TILE : (t + 1) * TILE] for rows_of in parts], axis=0)
        scores = lax.dot_general(queries, k_s[t], (((1,), (1,)), ((), ())), preferred_element_type=F32)
        weights = jnp.exp2(scores * (head_dim ** (-0.5) * LOG2E) + key_bias)
        inverse = head_totals(weights, rows, head_dim)
        mixed = jnp.dot(weights.astype(BF16), v_s[t], preferred_element_type=F32)
        for g in range(2):
            scale = jnp.where(half, inverse[2 * g], inverse[2 * g + 1])
            at = t * TILE + g * 128
            att[:, at : at + 128] = (mixed[:, g * 128 : (g + 1) * 128] * scale).astype(BF16)
    for at in range(0, width, TILE):
        acc = jnp.dot(att[...], out_w[slot, :, at : at + TILE], preferred_element_type=F32)
        for n, rows_of in enumerate(parts):
            before = x_s[rows_of, at : at + TILE].astype(F32)
            x_s[rows_of, at : at + TILE] = (before + acc[n * part : (n + 1) * part]).astype(BF16)


def own_kernel(head_dim, stage, own, qkv_w, norm_g, gains, head_ones, k_s, v_s, q_s, xn):
    @pl.when(lax.axis_index("section") == stage)
    def run():
        project_half(own, 0, 0, 0, head_dim, xn, k_s, v_s, q_s, qkv_w, norm_g, gains, head_ones)


def stage_kernel(head_dim, micro_count, stage, last_stage, layers, own, other, qkv_w, out_w, norm_g, gains, bias, head_ones, k_in, v_in, q_in, *refs):
    outs, (k_s, v_s, q_s, x_s, xn, att) = refs[:-6], refs[-6:]
    half_rows = own.shape[0]
    rows, part = 2 * half_rows, half_rows // 2
    slots = out_w.shape[0]

    @pl.when(lax.axis_index("section") == stage)
    def run():
        count = layers[0]
        seq, seq_count = lax.axis_index("seq"), lax.axis_size("seq")
        away = seq % 2 ^ seq // (seq_count // micro_count)
        x_s[0:half_rows, :] = own[...]
        x_s[half_rows:rows, :] = other[...]

        def one_slot(slot, carry):
            def one_half(n, carry):
                start = pl.multiple_of(n * half_rows, 16)
                project_half(x_s, start, start, slot, head_dim, xn, k_s, v_s, q_s, qkv_w, norm_g, gains, head_ones)
                return carry

            lax.fori_loop(jnp.where(slot == 0, 1, 0), 2, one_half, 0)
            key_bias = row_of(bias, slot, slots * min(stage, 1), slots)
            last = slot == count - 1

            def one_chunk(n, carry):
                if stage == 0:
                    starts = [jnp.where(last, half_rows * k + part * away, half_rows * n + part * k) for k in range(2)]
                else:
                    starts = [half_rows * n + part * k for k in range(2)]
                attend_rows(starts, part, key_bias, slot, head_dim, x_s, att, k_s, v_s, q_s, out_w)
                return carry

            lax.fori_loop(0, jnp.where(last, 1, 2), one_chunk, 0)
            return carry

        lax.fori_loop(0, count, one_slot, 0)
        piece = part // 2

        def some_rows(start, skip, size):
            whole = (skip + size + 15) // 16 * 16
            return x_s[pl.ds(start, whole), :].astype(F32)[skip : skip + size].astype(BF16)

        if last_stage:
            outs[0][...] = x_s[0:part, :]
        elif stage == 0:
            outs[0][...] = some_rows(pl.multiple_of(part * away, 16), 0, piece)
            outs[1][...] = x_s[pl.ds(pl.multiple_of(half_rows + part * away, 16), part), :]
        else:
            outs[0][...] = some_rows(0, 0, piece)
            outs[1][...] = some_rows(piece // 16 * 16, piece % 16, part)


def run_stage(stage, last_stage, layers, own, other, kept, head_dim, micro_count):
    qkv_w, out_w, norm_g, gains, bias, head_ones = (pltpu.with_memory_space_constraint(array, pltpu.VMEM) for array in kept)
    half_rows, width = own.shape
    rows, inner = 2 * half_rows, out_w.shape[1]
    whole = pl.BlockSpec(memory_space=pltpu.VMEM)
    small = pl.BlockSpec(memory_space=pltpu.SMEM)
    heads = (inner // TILE, TILE // head_dim * rows, TILE)
    made_shapes = [pltpu.VMEM(heads, BF16), pltpu.VMEM(heads, BF16), pltpu.VMEM((rows, inner), BF16)]
    made = pl.pallas_call(
        functools.partial(own_kernel, head_dim, stage),
        out_shape=made_shapes,
        in_specs=[whole] * 5,
        out_specs=[whole] * 3,
        scratch_shapes=[pltpu.VMEM((half_rows, width), BF16)],
        compiler_params=pltpu.CompilerParams(vmem_limit_bytes=8 * 2**20),
        cost_estimate=pl.CostEstimate(flops=6 * half_rows * width * inner, bytes_accessed=0, transcendentals=0),
        name="own_half",
    )(own, qkv_w, norm_g, gains, head_ones)
    made = [pltpu.with_memory_space_constraint(array, pltpu.VMEM) for array in made]
    outs = [half_rows // 2] if last_stage else [half_rows // 4, half_rows // 2]
    results = pl.pallas_call(
        functools.partial(stage_kernel, head_dim, micro_count, stage, last_stage),
        out_shape=[jax.ShapeDtypeStruct((size, width), BF16) for size in outs] + made_shapes,
        in_specs=[small] + [whole] * 11,
        out_specs=[whole] * (len(outs) + 3),
        scratch_shapes=[
            pltpu.VMEM((rows, width), BF16),
            pltpu.VMEM((half_rows, width), BF16),
            pltpu.VMEM((half_rows, inner), BF16),
        ],
        input_output_aliases={9 + n: len(outs) + n for n in range(3)},
        compiler_params=pltpu.CompilerParams(vmem_limit_bytes=12 * 2**20),
        name="stage",
    )(layers, own, other, qkv_w, out_w, norm_g, gains, bias, head_ones, *made)
    return results[: len(outs)]


def sent(value, seq_count, pairs):
    flat = [(a * seq_count + b, c * seq_count + d) for (a, b), (c, d) in pairs]
    return lax.ppermute(value, ("section", "seq"), flat)


def pair_local(latents, lengths, segment_layers, norm_gain, qkv_weight, qk_gain, out_weight):
    sections = lax.axis_size("section")
    seq_count = lax.axis_size("seq")
    chips = seq_count // 2
    micro_count, tok_rows, width = latents.shape
    section = lax.axis_index("section")
    seq = lax.axis_index("seq")
    core = seq % 2
    micro = seq // 2 // (chips // micro_count)
    seqs = range(seq_count)

    pieces = [lax.dynamic_index_in_dim(latents, micro, 0, False)]
    away = lax.dynamic_index_in_dim(latents, 1 - micro, 0, False)
    for k in range(1, chips):
        pairs = [(((0, 2, 3, 1)[k], s), (0, s ^ (2 * k))) for s in seqs]
        pieces.append(sent(pieces[0] if k < 2 else away, seq_count, pairs))
    qkv_kept, *kept, token = keep_weights(lengths, qkv_weight, norm_gain, qk_gain, seq_count * tok_rows)
    own = join_pieces(token, pieces)
    kept = [qkv_kept, keep_out(own, out_weight), *kept]

    for stage in range(sections):
        last = stage == sections - 1
        other = sent(own, seq_count, [((t, s), (t, s ^ 1)) for t in range(sections) for s in seqs])
        outs = run_stage(stage, last, segment_layers, own, other, kept, qk_gain.shape[1] // 2, micro_count)
        if not last:
            onward = [((stage, s), (stage + 1, s)) for s in seqs]
            around = [((t, s), ((t + 1) % sections, s)) for t in range(sections) for s in seqs]
            first, middle = sent(outs[0], seq_count, around), sent(outs[1], seq_count, onward)
            fourth = sent(first, seq_count, [((t, s), (t, s ^ 2)) for t in range(sections) for s in seqs])
            own = join_pieces(token, [first, middle, fourth])
    own = outs[0]

    final = sections - 1
    cols = width // sections

    def crosses(s):
        return s % 2 != s // (seq_count // micro_count)

    def target(s):
        return 2 * (s // 2 ^ (chips // 2 if crosses(s) else 0)) + s // (seq_count // micro_count)

    crossed = own[:, final * cols :]
    crossing = [s for s in seqs if crosses(s)]
    mine = None
    for t in range(final):
        here = sent(own[:, t * cols : (t + 1) * cols], seq_count, [((final, s), (t, target(s))) for s in seqs])
        mine = here if mine is None else jnp.where(section == t, here, mine)
    crossed = sent(crossed, seq_count, [((final, s), (final, target(s))) for s in crossing])
    stays = jnp.where(core == micro, own[:, final * cols :], crossed)
    mine = jnp.where(section == final, stays, mine)
    turned = micro == 1
    front = jnp.where(turned, mine[tok_rows:], mine[:tok_rows])
    back = jnp.where(turned, mine[:tok_rows], mine[tok_rows:])
    pairs = [((t, s), (t, s ^ 1)) for t in range(sections) for s in seqs]
    got = sent(jnp.where(core == 0, back, front), seq_count, pairs)
    return jnp.where(core == 0, jnp.stack([front, got]), jnp.stack([got, back]))


def local(latents, lengths, segment_layers, norm_gain, qkv_weight, qk_gain, out_weight):
    args = (latents, lengths, segment_layers, norm_gain, qkv_weight, qk_gain, out_weight)
    pairwise = lax.axis_size("seq") == 8 and latents.shape[0] == 2
    return pair_local(*args) if pairwise else relay_local(*args)


def solution(mesh):
    return jax.shard_map(
        local,
        mesh=mesh,
        in_specs=(
            P(None, "seq", None),
            P(),
            P("section"),
            P("section", None),
            P("section", None, None),
            P("section", None),
            P("section", None, None),
        ),
        out_specs=P(None, "seq", "section"),
        check_vma=False,
    )
```

profile of v0, /device:TPU:0, one launch (start us, length us, event | category | flops | bytes accessed | tf_op | source)
XLA Modules:
  0.0 98.4 jit_solution(3357841926993425437)
XLA Ops:
  0.0 1.0 dynamic-slice_bitcast_fusion
  1.0 1.3 %collective-permute-start = (bf16[40,1536]{1,0:T(8,128)(2,1)S(1)}, bf16[40,1536]{1,0:T(8,128)(2,1)S(1)}, u32[]{:S(2)}, u32[]{:S(2)}) collective-permute-start(bf16[40,1536]{1,0:T(8,128)(2,1)S(1)} %get-tuple-element.60.refs_0_), channel_id=1, source_target_pairs={{16,2},{17,3},{18,0},{19,1},{20,6},{21,7},{22,4},{23,5}} | collective-permute-start | bytes 368648 | tf_op jit(solution)/shard_map/ppermute | solution.py:417
  2.3 0.0 slice-start
  2.3 1.6 %collective-permute-start.1 = (bf16[40,1536]{1,0:T(8,128)(2,1)S(1)}, bf16[40,1536]{1,0:T(8,128)(2,1)S(1)}, u32[]{:S(2)}, u32[]{:S(2)}) collective-permute-start(bf16[40,1536]{1,0:T(8,128)(2,1)S(1)} %get-tuple-element.59), channel_id=1, source_target_pairs={{24,4},{25,5},{26,6},{27,7},{28,0},{29,1},{30,2},{31,3}} | collective-permute-start | bytes 368648 | tf_op jit(solution)/shard_map/ppermute | solution.py:417
  3.9 1.3 %collective-permute-start.2 = (bf16[40,1536]{1,0:T(8,128)(2,1)S(1)}, bf16[40,1536]{1,0:T(8,128)(2,1)S(1)}, u32[]{:S(2)}, u32[]{:S(2)}) collective-permute-start(bf16[40,1536]{1,0:T(8,128)(2,1)S(1)} %get-tuple-element.59), channel_id=1, source_target_pairs={{8,6},{9,7},{10,4},{11,5},{12,2},{13,3},{14,0},{15,1}} | collective-permute-start | bytes 368648 | tf_op jit(solution)/shard_map/ppermute | solution.py:417
  5.2 0.0 copy-start
  5.2 0.7 copy-done
  5.9 0.7 copy-done.1
  6.5 0.7 copy-done.2
  7.2 5.7 %keep_weights.1 = (bf16[2,1536,2304]{2,1,0:T(8,128)(2,1)S(1)}, f32[2,1536]{1,0:T(2,128)S(1)}, f32[4,256]{1,0:T(4,128)S(1)}, f32[4,1280]{1,0:T(4,128)S(1)}, bf16[...) custom-call(s32[2]{0:T(128)S(1)} %copy-done.1, bf16[2,1536,2304]{2,1,0:T(8,128)(2,1)} %qkv_hbm.1, ...), custom_call_target="tpu_custom_call" | custom-call | bytes 28311552 | tf_op jit(solution)/shard_map/keep_weights/pallas_call | solution.py:237
  12.9 0.0 collective-permute-done.refs_1_
  12.9 2.7 %collective-permute-done.1.refs_2_ = bf16[40,1536]{1,0:T(8,128)(2,1)S(1)} collective-permute-done((bf16[40,1536]{1,0:T(8,128)(2,1)S(1)}, bf16[40,1536]{1,0:T(8,128)(2,1)S(1)}, u32[]{:S(2)}, u32[]{:S(2)}) %collective-permute-start.1) | collective-permute-done | bytes 122912 | tf_op jit(solution)/shard_map/ppermute | solution.py:417
  15.6 0.0 collective-permute-done.2.refs_3_
  15.6 0.1 collective-permute-start.3
  16.4 0.3 keep_out.1.out_w
  16.7 1.8 %own_half.4 = (bf16[3,1280,256]{2,1,0:T(8,128)(2,1)S(1)}, bf16[3,1280,256]{2,1,0:T(8,128)(2,1)S(1)}, bf16[320,768]{1,0:T(8,128)(2,1)S(1)}) custom-call(bf16[160,1536]{1,0:T(8,128)(2,1)S(1)} %join_pieces.4.after.own, bf16[2,1536,2304]{2,1,0:T(8,128)(2,1)S(1)} %get-tuple-element.31.qkv_w, f32[2,1536]{1,0:T(2,128)S(1)} %get-tuple-element.32.norm_g, ...), custom_call_target="tpu_custom_call" | custom-call | flops 1132462080 | tf_op jit(solution)/shard_map/own_half/pallas_call | solution.py:386
  18.5 0.0 collective-permute-done.3.other
  18.5 10.7 %stage.4 = (bf16[40,1536]{1,0:T(8,128)(2,1)S(1)}, bf16[80,1536]{1,0:T(8,128)(2,1)S(1)}, bf16[3,1280,256]{2,1,0:T(8,128)(2,1)S(1)}, bf16[3,1280,256]{2,1,0:T(8,128)(2,1)S(1)}, bf16[320,768]{1,0:T(8,128)(2,1)S(1)}) custom-call(s32[1]{0:T(128)S(6)} %copy.32.layers, ...), custom_call_target="tpu_custom_call", output_to_operand_aliasing={{2}: (9, {}), {3}: (10, {}), {4}: (11, {})} | custom-call | tf_op jit(solution)/shard_map/stage/pallas_call | solution.py:398
  29.3 0.1 collective-permute-start.4
  29.3 1.3 %collective-permute-start.5 = (bf16[80,1536]{1,0:T(8,128)(2,1)S(1)}, bf16[80,1536]{1,0:T(8,128)(2,1)S(1)}, u32[]{:S(2)}, u32[]{:S(2)}) collective-permute-start(bf16[80,1536]{1,0:T(8,128)(2,1)S(1)} %get-tuple-element.40), channel_id=1, source_target_pairs={{0,8},{1,9},{2,10},{3,11},{4,12},{5,13},{6,14},{7,15}} | collective-permute-start | bytes 737288 | tf_op jit(solution)/shard_map/ppermute | solution.py:417
  30.6 5.3 %collective-permute-done.4.refs_0_ = bf16[40,1536]{1,0:T(8,128)(2,1)S(1)} collective-permute-done((bf16[40,1536]{1,0:T(8,128)(2,1)S(1)}, bf16[40,1536]{1,0:T(8,128)(2,1)S(1)}, u32[]{:S(2)}, u32[]{:S(2)}) %collective-permute-start.4) | collective-permute-done | bytes 122912 | tf_op jit(solution)/shard_map/ppermute | solution.py:417
  35.9 1.7 %collective-permute-start.6 = (bf16[40,1536]{1,0:T(8,128)(2,1)S(1)}, bf16[40,1536]{1,0:T(8,128)(2,1)S(1)}, u32[]{:S(2)}, u32[]{:S(2)}) collective-permute-start(bf16[40,1536]{1,0:T(8,128)(2,1)S(1)} %collective-permute-done.4.refs_0_), channel_id=1, source_target_pairs={{0,2},{1,3},{2,0},{3,1},{4,6},{5,7},{6,4},{7,5},{8,10},{9,11},{10,... | collective-permute-start | bytes 368648 | tf_op jit(solution)/shard_map/ppermute | solution.py:417
  37.7 3.2 %collective-permute-done.6.refs_2_ = bf16[40,1536]{1,0:T(8,128)(2,1)S(1)} collective-permute-done((bf16[40,1536]{1,0:T(8,128)(2,1)S(1)}, bf16[40,1536]{1,0:T(8,128)(2,1)S(1)}, u32[]{:S(2)}, u32[]{:S(2)}) %collective-permute-start.6) | collective-permute-done | bytes 122912 | tf_op jit(solution)/shard_map/ppermute | solution.py:417
  40.9 0.1 collective-permute-start.7
  41.0 1.8 %collective-permute-done.7.other = bf16[160,1536]{1,0:T(8,128)(2,1)S(1)} collective-permute-done((bf16[160,1536]{1,0:T(8,128)(2,1)S(1)}, bf16[160,1536]{1,0:T(8,128)(2,1)S(1)}, u32[]{:S(2)}, u32[]{:S(2)}) %collective-permute-start.7) | collective-permute-done | bytes 491552 | tf_op jit(solution)/shard_map/ppermute | solution.py:417
  42.8 3.4 %collective-permute-start.8 = (bf16[40,1536]{1,0:T(8,128)(2,1)S(1)}, bf16[40,1536]{1,0:T(8,128)(2,1)S(1)}, u32[]{:S(2)}, u32[]{:S(2)}) collective-permute-start(bf16[40,1536]{1,0:T(8,128)(2,1)S(1)} %get-tuple-element.44), channel_id=1, source_target_pairs={{0,8},{1,9},{2,10},{3,11},{4,12},{5,13},{6,14},{7,15},{8,16},{9,17... | collective-permute-start | bytes 368648 | tf_op jit(solution)/shard_map/ppermute | solution.py:417
  46.2 0.7 collective-permute-start.9
  46.9 2.5 %collective-permute-done.8.refs_0_ = bf16[40,1536]{1,0:T(8,128)(2,1)S(1)} collective-permute-done((bf16[40,1536]{1,0:T(8,128)(2,1)S(1)}, bf16[40,1536]{1,0:T(8,128)(2,1)S(1)}, u32[]{:S(2)}, u32[]{:S(2)}) %collective-permute-start.8) | collective-permute-done | bytes 122912 | tf_op jit(solution)/shard_map/ppermute | solution.py:417
  49.4 1.7 %collective-permute-start.10 = (bf16[40,1536]{1,0:T(8,128)(2,1)S(1)}, bf16[40,1536]{1,0:T(8,128)(2,1)S(1)}, u32[]{:S(2)}, u32[]{:S(2)}) collective-permute-start(bf16[40,1536]{1,0:T(8,128)(2,1)S(1)} %collective-permute-done.8.refs_0_), channel_id=1, source_target_pairs={{0,2},{1,3},{2,0},{3,1},{4,6},{5,7},{6,4},{7,5},{8,10},{9,11},{10,... | collective-permute-start | bytes 368648 | tf_op jit(solution)/shard_map/ppermute | solution.py:417
  51.2 3.2 %collective-permute-done.10.refs_2_ = bf16[40,1536]{1,0:T(8,128)(2,1)S(1)} collective-permute-done((bf16[40,1536]{1,0:T(8,128)(2,1)S(1)}, bf16[40,1536]{1,0:T(8,128)(2,1)S(1)}, u32[]{:S(2)}, u32[]{:S(2)}) %collective-permute-start.10) | collective-permute-done | bytes 122912 | tf_op jit(solution)/shard_map/ppermute | solution.py:417
  54.3 0.1 collective-permute-start.11
  54.4 0.2 own_half.6
  54.6 1.6 %collective-permute-done.11.other = bf16[160,1536]{1,0:T(8,128)(2,1)S(1)} collective-permute-done((bf16[160,1536]{1,0:T(8,128)(2,1)S(1)}, bf16[160,1536]{1,0:T(8,128)(2,1)S(1)}, u32[]{:S(2)}, u32[]{:S(2)}) %collective-permute-start.11) | collective-permute-done | bytes 491552 | tf_op jit(solution)/shard_map/ppermute | solution.py:417
  56.3 2.5 %collective-permute-start.12 = (bf16[40,1536]{1,0:T(8,128)(2,1)S(1)}, bf16[40,1536]{1,0:T(8,128)(2,1)S(1)}, u32[]{:S(2)}, u32[]{:S(2)}) collective-permute-start(bf16[40,1536]{1,0:T(8,128)(2,1)S(1)} %get-tuple-element.49), channel_id=1, source_target_pairs={{0,8},{1,9},{2,10},{3,11},{4,12},{5,13},{6,14},{7,15},{8,16},{9,17... | collective-permute-start | bytes 368648 | tf_op jit(solution)/shard_map/ppermute | solution.py:417
  58.8 0.7 collective-permute-start.13
  59.4 3.1 %collective-permute-done.12.refs_0_ = bf16[40,1536]{1,0:T(8,128)(2,1)S(1)} collective-permute-done((bf16[40,1536]{1,0:T(8,128)(2,1)S(1)}, bf16[40,1536]{1,0:T(8,128)(2,1)S(1)}, u32[]{:S(2)}, u32[]{:S(2)}) %collective-permute-start.12) | collective-permute-done | bytes 122912 | tf_op jit(solution)/shard_map/ppermute | solution.py:417
  62.5 1.7 %collective-permute-start.14 = (bf16[40,1536]{1,0:T(8,128)(2,1)S(1)}, bf16[40,1536]{1,0:T(8,128)(2,1)S(1)}, u32[]{:S(2)}, u32[]{:S(2)}) collective-permute-start(bf16[40,1536]{1,0:T(8,128)(2,1)S(1)} %collective-permute-done.12.refs_0_), channel_id=1, source_target_pairs={{0,2},{1,3},{2,0},{3,1},{4,6},{5,7},{6,4},{7,5},{8,10},{9,11},{10,... | collective-permute-start | bytes 368648 | tf_op jit(solution)/shard_map/ppermute | solution.py:417
  64.3 3.2 %collective-permute-done.14.refs_2_ = bf16[40,1536]{1,0:T(8,128)(2,1)S(1)} collective-permute-done((bf16[40,1536]{1,0:T(8,128)(2,1)S(1)}, bf16[40,1536]{1,0:T(8,128)(2,1)S(1)}, u32[]{:S(2)}, u32[]{:S(2)}) %collective-permute-start.14) | collective-permute-done | bytes 122912 | tf_op jit(solution)/shard_map/ppermute | solution.py:417
  67.5 0.1 collective-permute-start.15
  67.6 1.8 %collective-permute-done.15.other = bf16[160,1536]{1,0:T(8,128)(2,1)S(1)} collective-permute-done((bf16[160,1536]{1,0:T(8,128)(2,1)S(1)}, bf16[160,1536]{1,0:T(8,128)(2,1)S(1)}, u32[]{:S(2)}, u32[]{:S(2)}) %collective-permute-start.15) | collective-permute-done | bytes 491552 | tf_op jit(solution)/shard_map/ppermute | solution.py:417
  69.4 0.7 collective-permute-start.16
  70.1 0.7 collective-permute-start.17
  70.8 0.7 collective-permute-start.18
  71.4 1.3 %collective-permute-start.19 = (bf16[80,384]{1,0:T(8,128)(2,1)S(1)}, bf16[80,384]{1,0:T(8,128)(2,1)S(1)}, u32[]{:S(2)}, u32[]{:S(2)}) collective-permute-start(bf16[80,384]{1,0:T(8,128)(2,1)S(1)} %get-tuple-element.56), channel_id=1, source_target_pairs={{24,0},{25,4},{26,2},{27,6},{28,1},{29,5},{30,3},{31,7}} | collective-permute-start | bytes 184328 | tf_op jit(solution)/shard_map/ppermute | solution.py:417
  72.8 19.9 %collective-permute-done.19 = bf16[80,384]{1,0:T(8,128)(2,1)S(1)} collective-permute-done((bf16[80,384]{1,0:T(8,128)(2,1)S(1)}, bf16[80,384]{1,0:T(8,128)(2,1)S(1)}, u32[]{:S(2)}, u32[]{:S(2)}) %collective-permute-start.19) | collective-permute-done | bytes 61472 | tf_op jit(solution)/shard_map/ppermute | solution.py:417
  92.7 4.2 %collective-permute-start.20 = (bf16[40,384]{1,0:T(8,128)(2,1)S(1)}, bf16[40,384]{1,0:T(8,128)(2,1)S(1)}, u32[]{:S(2)}, u32[]{:S(2)}) collective-permute-start(bf16[40,384]{1,0:T(8,128)(2,1)S(1)} %get-tuple-element.62), channel_id=1, source_target_pairs={{0,1},{1,0},{2,3},{3,2},{4,5},{5,4},{6,7},{7,6},{8,9},{9,8},{10,11... | collective-permute-start | bytes 92168 | tf_op jit(solution)/shard_map/ppermute | solution.py:417
  96.9 0.9 collective-permute-done.20
  97.7 0.6 maximum_select_fusion
  (24 shorter events, 0.3 us)
Async XLA Ops:
  1.0 11.9 %collective-permute-start = (bf16[40,1536]{1,0:T(8,128)(2,1)S(1)}, bf16[40,1536]{1,0:T(8,128)(2,1)S(1)}, u32[]{:S(2)}, u32[]{:S(2)}) collective-permute-start(bf16[40,1536]{1,0:T(8,128)(2,1)S(1)} %get-tuple-element.60.refs_0_), channel_id=1, source_target_pairs={{16,2},{17,3},{18,0},{19,1},{20,6},{21,7},{22,4},{23,5}} | collective-permute-start | bytes 368648 | tf_op jit(solution)/shard_map/ppermute | solution.py:417
  2.3 14.1 %slice-start = ((s8[4718592]{0:T(1024)(128)(4,1)}), s8[4194304]{0:T(1024)(128)(4,1)S(1)}, s32[]{:S(2)}) async-start(s8[4718592]{0:T(1024)(128)(4,1)} %bitcast.9), calls=%async_computation | async-start | bytes 8388608
  2.3 14.1 %slice-start.1 = ((s8[4718592]{0:T(1024)(128)(4,1)}), s8[524288]{0:T(1024)(128)(4,1)S(1)}, s32[]{:S(2)}) async-start(s8[4718592]{0:T(1024)(128)(4,1)} %bitcast.9), calls=%async_computation.1 | async-start | bytes 1048576
  2.3 13.3 %collective-permute-start.1 = (bf16[40,1536]{1,0:T(8,128)(2,1)S(1)}, bf16[40,1536]{1,0:T(8,128)(2,1)S(1)}, u32[]{:S(2)}, u32[]{:S(2)}) collective-permute-start(bf16[40,1536]{1,0:T(8,128)(2,1)S(1)} %get-tuple-element.59), channel_id=1, source_target_pairs={{24,4},{25,5},{26,6},{27,7},{28,0},{29,1},{30,2},{31,3}} | collective-permute-start | bytes 368648 | tf_op jit(solution)/shard_map/ppermute | solution.py:417
  3.9 11.7 %collective-permute-start.2 = (bf16[40,1536]{1,0:T(8,128)(2,1)S(1)}, bf16[40,1536]{1,0:T(8,128)(2,1)S(1)}, u32[]{:S(2)}, u32[]{:S(2)}) collective-permute-start(bf16[40,1536]{1,0:T(8,128)(2,1)S(1)} %get-tuple-element.59), channel_id=1, source_target_pairs={{8,6},{9,7},{10,4},{11,5},{12,2},{13,3},{14,0},{15,1}} | collective-permute-start | bytes 368648 | tf_op jit(solution)/shard_map/ppermute | solution.py:417
  5.2 0.7 copy-start
  5.9 0.7 copy-start.1
  6.5 0.7 copy-start.2
  15.6 2.9 %collective-permute-start.3 = (bf16[160,1536]{1,0:T(8,128)(2,1)S(1)}, bf16[160,1536]{1,0:T(8,128)(2,1)S(1)}, u32[]{:S(2)}, u32[]{:S(2)}) collective-permute-start(bf16[160,1536]{1,0:T(8,128)(2,1)S(1)} %join_pieces.4.after.own), channel_id=1, source_target_pairs={{0,1},{1,0},{2,3},{3,2},{4,5},{5,4},{6,7},{7,6},{8,9},{9,8},{10,11... | collective-permute-start | bytes 1474568 | tf_op jit(solution)/shard_map/ppermute | solution.py:417
  29.3 6.7 %collective-permute-start.4 = (bf16[40,1536]{1,0:T(8,128)(2,1)S(1)}, bf16[40,1536]{1,0:T(8,128)(2,1)S(1)}, u32[]{:S(2)}, u32[]{:S(2)}) collective-permute-start(bf16[40,1536]{1,0:T(8,128)(2,1)S(1)} %get-tuple-element.39), channel_id=1, source_target_pairs={{0,8},{1,9},{2,10},{3,11},{4,12},{5,13},{6,14},{7,15},{8,16},{9,17... | collective-permute-start | bytes 368648 | tf_op jit(solution)/shard_map/ppermute | solution.py:417
  29.3 11.6 %collective-permute-start.5 = (bf16[80,1536]{1,0:T(8,128)(2,1)S(1)}, bf16[80,1536]{1,0:T(8,128)(2,1)S(1)}, u32[]{:S(2)}, u32[]{:S(2)}) collective-permute-start(bf16[80,1536]{1,0:T(8,128)(2,1)S(1)} %get-tuple-element.40), channel_id=1, source_target_pairs={{0,8},{1,9},{2,10},{3,11},{4,12},{5,13},{6,14},{7,15}} | collective-permute-start | bytes 737288 | tf_op jit(solution)/shard_map/ppermute | solution.py:417
  35.9 4.9 %collective-permute-start.6 = (bf16[40,1536]{1,0:T(8,128)(2,1)S(1)}, bf16[40,1536]{1,0:T(8,128)(2,1)S(1)}, u32[]{:S(2)}, u32[]{:S(2)}) collective-permute-start(bf16[40,1536]{1,0:T(8,128)(2,1)S(1)} %collective-permute-done.4.refs_0_), channel_id=1, source_target_pairs={{0,2},{1,3},{2,0},{3,1},{4,6},{5,7},{6,4},{7,5},{8,10},{9,11},{10,... | collective-permute-start | bytes 368648 | tf_op jit(solution)/shard_map/ppermute | solution.py:417
  40.9 1.9 %collective-permute-start.7 = (bf16[160,1536]{1,0:T(8,128)(2,1)S(1)}, bf16[160,1536]{1,0:T(8,128)(2,1)S(1)}, u32[]{:S(2)}, u32[]{:S(2)}) collective-permute-start(bf16[160,1536]{1,0:T(8,128)(2,1)S(1)} %join_pieces.5.own), channel_id=1, source_target_pairs={{0,1},{1,0},{2,3},{3,2},{4,5},{5,4},{6,7},{7,6},{8,9},{9,8},{10,11... | collective-permute-start | bytes 1474568 | tf_op jit(solution)/shard_map/ppermute | solution.py:417
  42.8 6.6 %collective-permute-start.8 = (bf16[40,1536]{1,0:T(8,128)(2,1)S(1)}, bf16[40,1536]{1,0:T(8,128)(2,1)S(1)}, u32[]{:S(2)}, u32[]{:S(2)}) collective-permute-start(bf16[40,1536]{1,0:T(8,128)(2,1)S(1)} %get-tuple-element.44), channel_id=1, source_target_pairs={{0,8},{1,9},{2,10},{3,11},{4,12},{5,13},{6,14},{7,15},{8,16},{9,17... | collective-permute-start | bytes 368648 | tf_op jit(solution)/shard_map/ppermute | solution.py:417
  46.2 8.1 %collective-permute-start.9 = (bf16[80,1536]{1,0:T(8,128)(2,1)S(1)}, bf16[80,1536]{1,0:T(8,128)(2,1)S(1)}, u32[]{:S(2)}, u32[]{:S(2)}) collective-permute-start(bf16[80,1536]{1,0:T(8,128)(2,1)S(1)} %get-tuple-element.45), channel_id=1, source_target_pairs={{8,16},{9,17},{10,18},{11,19},{12,20},{13,21},{14,22},{15,23}} | collective-permute-start | bytes 737288 | tf_op jit(solution)/shard_map/ppermute | solution.py:417
  49.4 4.9 %collective-permute-start.10 = (bf16[40,1536]{1,0:T(8,128)(2,1)S(1)}, bf16[40,1536]{1,0:T(8,128)(2,1)S(1)}, u32[]{:S(2)}, u32[]{:S(2)}) collective-permute-start(bf16[40,1536]{1,0:T(8,128)(2,1)S(1)} %collective-permute-done.8.refs_0_), channel_id=1, source_target_pairs={{0,2},{1,3},{2,0},{3,1},{4,6},{5,7},{6,4},{7,5},{8,10},{9,11},{10,... | collective-permute-start | bytes 368648 | tf_op jit(solution)/shard_map/ppermute | solution.py:417
  54.3 1.9 %collective-permute-start.11 = (bf16[160,1536]{1,0:T(8,128)(2,1)S(1)}, bf16[160,1536]{1,0:T(8,128)(2,1)S(1)}, u32[]{:S(2)}, u32[]{:S(2)}) collective-permute-start(bf16[160,1536]{1,0:T(8,128)(2,1)S(1)} %join_pieces.6.own), channel_id=1, source_target_pairs={{0,1},{1,0},{2,3},{3,2},{4,5},{5,4},{6,7},{7,6},{8,9},{9,8},{10,11... | collective-permute-start | bytes 1474568 | tf_op jit(solution)/shard_map/ppermute | solution.py:417
  56.3 6.3 %collective-permute-start.12 = (bf16[40,1536]{1,0:T(8,128)(2,1)S(1)}, bf16[40,1536]{1,0:T(8,128)(2,1)S(1)}, u32[]{:S(2)}, u32[]{:S(2)}) collective-permute-start(bf16[40,1536]{1,0:T(8,128)(2,1)S(1)} %get-tuple-element.49), channel_id=1, source_target_pairs={{0,8},{1,9},{2,10},{3,11},{4,12},{5,13},{6,14},{7,15},{8,16},{9,17... | collective-permute-start | bytes 368648 | tf_op jit(solution)/shard_map/ppermute | solution.py:417
  58.8 8.7 %collective-permute-start.13 = (bf16[80,1536]{1,0:T(8,128)(2,1)S(1)}, bf16[80,1536]{1,0:T(8,128)(2,1)S(1)}, u32[]{:S(2)}, u32[]{:S(2)}) collective-permute-start(bf16[80,1536]{1,0:T(8,128)(2,1)S(1)} %get-tuple-element.50), channel_id=1, source_target_pairs={{16,24},{17,25},{18,26},{19,27},{20,28},{21,29},{22,30},{23,31}} | collective-permute-start | bytes 737288 | tf_op jit(solution)/shard_map/ppermute | solution.py:417
  62.5 4.9 %collective-permute-start.14 = (bf16[40,1536]{1,0:T(8,128)(2,1)S(1)}, bf16[40,1536]{1,0:T(8,128)(2,1)S(1)}, u32[]{:S(2)}, u32[]{:S(2)}) collective-permute-start(bf16[40,1536]{1,0:T(8,128)(2,1)S(1)} %collective-permute-done.12.refs_0_), channel_id=1, source_target_pairs={{0,2},{1,3},{2,0},{3,1},{4,6},{5,7},{6,4},{7,5},{8,10},{9,11},{10,... | collective-permute-start | bytes 368648 | tf_op jit(solution)/shard_map/ppermute | solution.py:417
  67.5 1.9 %collective-permute-start.15 = (bf16[160,1536]{1,0:T(8,128)(2,1)S(1)}, bf16[160,1536]{1,0:T(8,128)(2,1)S(1)}, u32[]{:S(2)}, u32[]{:S(2)}) collective-permute-start(bf16[160,1536]{1,0:T(8,128)(2,1)S(1)} %join_pieces.7.own), channel_id=1, source_target_pairs={{0,1},{1,0},{2,3},{3,2},{4,5},{5,4},{6,7},{7,6},{8,9},{9,8},{10,11... | collective-permute-start | bytes 1474568 | tf_op jit(solution)/shard_map/ppermute | solution.py:417
  69.4 3.3 %collective-permute-start.16 = (bf16[80,384]{1,0:T(8,128)(2,1)S(1)}, bf16[80,384]{1,0:T(8,128)(2,1)S(1)}, u32[]{:S(2)}, u32[]{:S(2)}) collective-permute-start(bf16[80,384]{1,0:T(8,128)(2,1)S(1)} %get-tuple-element.55), channel_id=1, source_target_pairs={{25,28},{27,30},{28,25},{30,27}} | collective-permute-start | bytes 184328 | tf_op jit(solution)/shard_map/ppermute | solution.py:417
  70.1 2.7 %collective-permute-start.17 = (bf16[80,384]{1,0:T(8,128)(2,1)S(1)}, bf16[80,384]{1,0:T(8,128)(2,1)S(1)}, u32[]{:S(2)}, u32[]{:S(2)}) collective-permute-start(bf16[80,384]{1,0:T(8,128)(2,1)S(1)} %get-tuple-element.58), channel_id=1, source_target_pairs={{24,16},{25,20},{26,18},{27,22},{28,17},{29,21},{30,19},{31,23}} | collective-permute-start | bytes 184328 | tf_op jit(solution)/shard_map/ppermute | solution.py:417
  70.8 2.0 %collective-permute-start.18 = (bf16[80,384]{1,0:T(8,128)(2,1)S(1)}, bf16[80,384]{1,0:T(8,128)(2,1)S(1)}, u32[]{:S(2)}, u32[]{:S(2)}) collective-permute-start(bf16[80,384]{1,0:T(8,128)(2,1)S(1)} %get-tuple-element.57), channel_id=1, source_target_pairs={{24,8},{25,12},{26,10},{27,14},{28,9},{29,13},{30,11},{31,15}} | collective-permute-start | bytes 184328 | tf_op jit(solution)/shard_map/ppermute | solution.py:417
  71.4 21.2 %collective-permute-start.19 = (bf16[80,384]{1,0:T(8,128)(2,1)S(1)}, bf16[80,384]{1,0:T(8,128)(2,1)S(1)}, u32[]{:S(2)}, u32[]{:S(2)}) collective-permute-start(bf16[80,384]{1,0:T(8,128)(2,1)S(1)} %get-tuple-element.56), channel_id=1, source_target_pairs={{24,0},{25,4},{26,2},{27,6},{28,1},{29,5},{30,3},{31,7}} | collective-permute-start | bytes 184328 | tf_op jit(solution)/shard_map/ppermute | solution.py:417
  92.7 5.0 %collective-permute-start.20 = (bf16[40,384]{1,0:T(8,128)(2,1)S(1)}, bf16[40,384]{1,0:T(8,128)(2,1)S(1)}, u32[]{:S(2)}, u32[]{:S(2)}) collective-permute-start(bf16[40,384]{1,0:T(8,128)(2,1)S(1)} %get-tuple-element.62), channel_id=1, source_target_pairs={{0,1},{1,0},{2,3},{3,2},{4,5},{5,4},{6,7},{7,6},{8,9},{9,8},{10,11... | collective-permute-start | bytes 92168 | tf_op jit(solution)/shard_map/ppermute | solution.py:417
where the time goes:
time: 98.7 us; the launch traced here: 98.4 us
  waiting for transfers between devices  49.2 us (50%)
  starting transfers between devices  25.6 us (26%)
  Pallas kernels  18.9 us (19%)
  local copies, waits for them, and re-layouts  3.01 us (3%)
  between operations  0.99 us (1%)
    ppermute x21, waiting for transfers between devices, sent(): return lax.ppermute(value, ('section', 'seq'), flat)  49.2 us
    ppermute x21, starting transfers between devices, sent(): return lax.ppermute(value, ('section', 'seq'), flat)  25.6 us
    pallas_call x4, Pallas kernels, run_stage(): pl.pallas_call(functools.partial(stage_kernel, head_dim, micro_count, sta...  10.7 us
    pallas_call x1, Pallas kernels, keep_weights(): pl.pallas_call(functools.partial(keep_kernel, head_dim), out_shape=[pltpu...  5.69 us
    pallas_call x4, Pallas kernels, run_stage(): pl.pallas_call(functools.partial(own_kernel, head_dim, stage), out_shape=...  2.01 us
    unnamed x10, local copies, waits for them, and re-layouts  2.01 us
  transfers between devices with their start and end apart: 21, of which 12 were waited for; matrix products, arithmetic and copies ran while one was open for 0% of the time, Pallas kernels for 8%

commit v1 on v0

--- a/solution.py
+++ b/solution.py
@@ -173,7 +173,7 @@
     return totals
 
 
-def keep_kernel(head_dim, lengths, qkv_hbm, norm_gain, qk_gain, qkv_w, norm_g, gains, bias, head_ones, token, sem):
+def keep_kernel(head_dim, lengths, layers, qkv_hbm, norm_gain, qk_gain, qkv_w, norm_g, gains, bias, head_ones, token, sem):
     copy = pltpu.make_async_copy(qkv_hbm, qkv_w, sem)
     copy.start()
     slots = norm_gain.shape[0]
@@ -229,7 +229,7 @@
     )(after, out_w)
 
 
-def keep_weights(lengths, qkv_w, norm_gain, qk_gain, rows):
+def keep_weights(lengths, layers, qkv_w, norm_gain, qk_gain, rows):
     far = pl.BlockSpec(memory_space=pltpu.HBM)
     whole = pl.BlockSpec(memory_space=pltpu.VMEM)
     small = pl.BlockSpec(memory_space=pltpu.SMEM)
@@ -244,13 +244,13 @@
             pltpu.VMEM((TILE, TILE), BF16),
             pltpu.VMEM((8, 128), F32),
         ],
-        in_specs=[small, far, whole, whole],
+        in_specs=[small, small, far, whole, whole],
         out_specs=[whole] * 6,
         scratch_shapes=[pltpu.SemaphoreType.DMA],
         compiler_params=pltpu.CompilerParams(vmem_limit_bytes=40 * 2**20),
         cost_estimate=pl.CostEstimate(flops=0, bytes_accessed=4 * qkv_w.size, transcendentals=0),
         name="keep_weights",
-    )(lengths, qkv_w, norm_gain, qk_gain)
+    )(lengths, layers, qkv_w, norm_gain, qk_gain)
 
 
 def join_kernel(token, *refs):
@@ -433,9 +433,9 @@
     for k in range(1, chips):
         pairs = [(((0, 2, 3, 1)[k], s), (0, s ^ (2 * k))) for s in seqs]
         pieces.append(sent(pieces[0] if k < 2 else away, seq_count, pairs))
-    qkv_kept, *kept, token = keep_weights(lengths, qkv_weight, norm_gain, qk_gain, seq_count * tok_rows)
+    qkv_kept, *kept, token = keep_weights(lengths, segment_layers, qkv_weight, norm_gain, qk_gain, seq_count * tok_rows)
+    kept = [qkv_kept, keep_out(token, out_weight), *kept]
     own = join_pieces(token, pieces)
-    kept = [qkv_kept, keep_out(own, out_weight), *kept]
 
     for stage in range(sections):
         last = stage == sections - 1

time: 98.7 us -> 97.7 us (0.990)
  waiting for transfers between devices: 49.2 us -> 47.9 us
    ppermute x21, waiting for transfers between devices: 49.2 us -> 47.9 us  [sent(): return lax.ppermute(value, ('section', 'seq'), flat)]
where the time goes in v1:
time: 97.7 us; the launch traced here: 97.4 us
  waiting for transfers between devices  47.9 us (49%)
  starting transfers between devices  25.7 us (26%)
  Pallas kernels  18.9 us (19%)
  local copies, waits for them, and re-layouts  3.18 us (3%)
  between operations  1.13 us (1%)
    ppermute x21, waiting for transfers between devices, sent(): return lax.ppermute(value, ('section', 'seq'), flat)  47.9 us
    ppermute x21, starting transfers between devices, sent(): return lax.ppermute(value, ('section', 'seq'), flat)  25.7 us
    pallas_call x4, Pallas kernels, run_stage(): pl.pallas_call(functools.partial(stage_kernel, head_dim, micro_count, sta...  10.7 us
    pallas_call x1, Pallas kernels, keep_weights(): pl.pallas_call(functools.partial(keep_kernel, head_dim), out_shape=[pltpu...  5.69 us
    unnamed x10, local copies, waits for them, and re-layouts  2.17 us
    pallas_call x4, Pallas kernels, run_stage(): pl.pallas_call(functools.partial(own_kernel, head_dim, stage), out_shape=...  2.01 us
  transfers between devices with their start and end apart: 21, of which 12 were waited for; matrix products, arithmetic and copies ran while one was open for 0% of the time, Pallas kernels for 8%

profile of v1, /device:TPU:0, one launch (start us, length us, event | category | flops | bytes accessed | tf_op | source)
XLA Modules:
  0.0 97.4 jit_solution(14167391278755377923)
XLA Ops:
  0.0 1.0 %dynamic-slice_bitcast_fusion = (bf16[40,1536]{1,0:T(8,128)(2,1)S(1)}, bf16[40,1536]{1,0:T(8,128)(2,1)S(1)}) fusion(bf16[2,40,1536]{2,1,0:T(8,128)(2,1)} %param.7, s32[]{:T(128)S(6)} %select_n.81, s32[]{:T(128)S(6)} %select_n.80), kind=kLoop, calls=%fused_computation | loop fusion | bytes 491528 | tf_op jit(solution)/shard_map/jit(dynamic_index_in_dim)/squeeze | solution.py:432
  1.0 1.3 %collective-permute-start = (bf16[40,1536]{1,0:T(8,128)(2,1)S(1)}, bf16[40,1536]{1,0:T(8,128)(2,1)S(1)}, u32[]{:S(2)}, u32[]{:S(2)}) collective-permute-start(bf16[40,1536]{1,0:T(8,128)(2,1)S(1)} %get-tuple-element.60.refs_0_), channel_id=1, source_target_pairs={{16,2},{17,3},{18,0},{19,1},{20,6},{21,7},{22,4},{23,5}} | collective-permute-start | bytes 368648 | tf_op jit(solution)/shard_map/ppermute | solution.py:417
  2.3 1.3 %collective-permute-start.1 = (bf16[40,1536]{1,0:T(8,128)(2,1)S(1)}, bf16[40,1536]{1,0:T(8,128)(2,1)S(1)}, u32[]{:S(2)}, u32[]{:S(2)}) collective-permute-start(bf16[40,1536]{1,0:T(8,128)(2,1)S(1)} %get-tuple-element.59), channel_id=1, source_target_pairs={{24,4},{25,5},{26,6},{27,7},{28,0},{29,1},{30,2},{31,3}} | collective-permute-start | bytes 368648 | tf_op jit(solution)/shard_map/ppermute | solution.py:417
  3.6 1.3 %collective-permute-start.2 = (bf16[40,1536]{1,0:T(8,128)(2,1)S(1)}, bf16[40,1536]{1,0:T(8,128)(2,1)S(1)}, u32[]{:S(2)}, u32[]{:S(2)}) collective-permute-start(bf16[40,1536]{1,0:T(8,128)(2,1)S(1)} %get-tuple-element.59), channel_id=1, source_target_pairs={{8,6},{9,7},{10,4},{11,5},{12,2},{13,3},{14,0},{15,1}} | collective-permute-start | bytes 368648 | tf_op jit(solution)/shard_map/ppermute | solution.py:417
  4.9 0.0 slice-start
  5.7 0.0 copy-start
  5.7 0.8 copy-done
  6.6 0.7 copy-done.1
  7.2 0.7 copy-done.2
  7.9 5.7 %keep_weights.1 = (bf16[2,1536,2304]{2,1,0:T(8,128)(2,1)S(1)}, f32[2,1536]{1,0:T(2,128)S(1)}, f32[4,256]{1,0:T(4,128)S(1)}, f32[4,1280]{1,0:T(4,128)S(1)}, bf16[...) custom-call(s32[2]{0:T(128)S(1)} %copy-done.1, s32[1]{0:T(128)S(6)} %copy.32.layers, bf16[2,1536,2304]{2,1,0:T(8,128)(2,1)} %qkv_hbm.1, ...), custom_call_target="tpu_custom_call" | custom-call | bytes 28311552 | tf_op jit(solution)/shard_map/keep_weights/pallas_call | solution.py:237
  13.6 0.0 collective-permute-done.refs_1_
  13.6 1.6 %collective-permute-done.1.refs_2_ = bf16[40,1536]{1,0:T(8,128)(2,1)S(1)} collective-permute-done((bf16[40,1536]{1,0:T(8,128)(2,1)S(1)}, bf16[40,1536]{1,0:T(8,128)(2,1)S(1)}, u32[]{:S(2)}, u32[]{:S(2)}) %collective-permute-start.1) | collective-permute-done | bytes 122912 | tf_op jit(solution)/shard_map/ppermute | solution.py:417
  15.2 0.1 collective-permute-start.3
  15.3 0.3 keep_out.1.out_w
  15.7 1.8 %own_half.4 = (bf16[3,1280,256]{2,1,0:T(8,128)(2,1)S(1)}, bf16[3,1280,256]{2,1,0:T(8,128)(2,1)S(1)}, bf16[320,768]{1,0:T(8,128)(2,1)S(1)}) custom-call(bf16[160,1536]{1,0:T(8,128)(2,1)S(1)} %join_pieces.4.own, bf16[2,1536,2304]{2,1,0:T(8,128)(2,1)S(1)} %get-tuple-element.31.qkv_w, f32[2,1536]{1,0:T(2,128)S(1)} %get-tuple-element.32.norm_g, ...), custom_call_target="tpu_custom_call" | custom-call | flops 1132462080 | tf_op jit(solution)/shard_map/own_half/pallas_call | solution.py:386
  17.5 0.0 collective-permute-done.3.other
  17.5 10.7 %stage.4 = (bf16[40,1536]{1,0:T(8,128)(2,1)S(1)}, bf16[80,1536]{1,0:T(8,128)(2,1)S(1)}, bf16[3,1280,256]{2,1,0:T(8,128)(2,1)S(1)}, bf16[3,1280,256]{2,1,0:T(8,128)(2,1)S(1)}, bf16[320,768]{1,0:T(8,128)(2,1)S(1)}) custom-call(s32[1]{0:T(128)S(6)} %copy.32.layers, ...), custom_call_target="tpu_custom_call", output_to_operand_aliasing={{2}: (9, {}), {3}: (10, {}), {4}: (11, {})} | custom-call | tf_op jit(solution)/shard_map/stage/pallas_call | solution.py:398
  28.2 0.1 collective-permute-start.4
  28.3 1.3 %collective-permute-start.5 = (bf16[80,1536]{1,0:T(8,128)(2,1)S(1)}, bf16[80,1536]{1,0:T(8,128)(2,1)S(1)}, u32[]{:S(2)}, u32[]{:S(2)}) collective-permute-start(bf16[80,1536]{1,0:T(8,128)(2,1)S(1)} %get-tuple-element.40), channel_id=1, source_target_pairs={{0,8},{1,9},{2,10},{3,11},{4,12},{5,13},{6,14},{7,15}} | collective-permute-start | bytes 737288 | tf_op jit(solution)/shard_map/ppermute | solution.py:417
  29.6 5.3 %collective-permute-done.4.refs_0_ = bf16[40,1536]{1,0:T(8,128)(2,1)S(1)} collective-permute-done((bf16[40,1536]{1,0:T(8,128)(2,1)S(1)}, bf16[40,1536]{1,0:T(8,128)(2,1)S(1)}, u32[]{:S(2)}, u32[]{:S(2)}) %collective-permute-start.4) | collective-permute-done | bytes 122912 | tf_op jit(solution)/shard_map/ppermute | solution.py:417
  34.8 1.9 %collective-permute-start.6 = (bf16[40,1536]{1,0:T(8,128)(2,1)S(1)}, bf16[40,1536]{1,0:T(8,128)(2,1)S(1)}, u32[]{:S(2)}, u32[]{:S(2)}) collective-permute-start(bf16[40,1536]{1,0:T(8,128)(2,1)S(1)} %collective-permute-done.4.refs_0_), channel_id=1, source_target_pairs={{0,2},{1,3},{2,0},{3,1},{4,6},{5,7},{6,4},{7,5},{8,10},{9,11},{10,... | collective-permute-start | bytes 368648 | tf_op jit(solution)/shard_map/ppermute | solution.py:417
  36.7 3.2 %collective-permute-done.6.refs_2_ = bf16[40,1536]{1,0:T(8,128)(2,1)S(1)} collective-permute-done((bf16[40,1536]{1,0:T(8,128)(2,1)S(1)}, bf16[40,1536]{1,0:T(8,128)(2,1)S(1)}, u32[]{:S(2)}, u32[]{:S(2)}) %collective-permute-start.6) | collective-permute-done | bytes 122912 | tf_op jit(solution)/shard_map/ppermute | solution.py:417
  39.9 0.0 collective-permute-done.5.refs_1_
  39.9 0.1 collective-permute-start.7
  40.0 1.8 %collective-permute-done.7.other = bf16[160,1536]{1,0:T(8,128)(2,1)S(1)} collective-permute-done((bf16[160,1536]{1,0:T(8,128)(2,1)S(1)}, bf16[160,1536]{1,0:T(8,128)(2,1)S(1)}, u32[]{:S(2)}, u32[]{:S(2)}) %collective-permute-start.7) | collective-permute-done | bytes 491552 | tf_op jit(solution)/shard_map/ppermute | solution.py:417
  41.8 3.3 %collective-permute-start.8 = (bf16[40,1536]{1,0:T(8,128)(2,1)S(1)}, bf16[40,1536]{1,0:T(8,128)(2,1)S(1)}, u32[]{:S(2)}, u32[]{:S(2)}) collective-permute-start(bf16[40,1536]{1,0:T(8,128)(2,1)S(1)} %get-tuple-element.44), channel_id=1, source_target_pairs={{0,8},{1,9},{2,10},{3,11},{4,12},{5,13},{6,14},{7,15},{8,16},{9,17... | collective-permute-start | bytes 368648 | tf_op jit(solution)/shard_map/ppermute | solution.py:417
  45.1 0.7 collective-permute-start.9
  45.8 2.5 %collective-permute-done.8.refs_0_ = bf16[40,1536]{1,0:T(8,128)(2,1)S(1)} collective-permute-done((bf16[40,1536]{1,0:T(8,128)(2,1)S(1)}, bf16[40,1536]{1,0:T(8,128)(2,1)S(1)}, u32[]{:S(2)}, u32[]{:S(2)}) %collective-permute-start.8) | collective-permute-done | bytes 122912 | tf_op jit(solution)/shard_map/ppermute | solution.py:417
  48.3 1.9 %collective-permute-start.10 = (bf16[40,1536]{1,0:T(8,128)(2,1)S(1)}, bf16[40,1536]{1,0:T(8,128)(2,1)S(1)}, u32[]{:S(2)}, u32[]{:S(2)}) collective-permute-start(bf16[40,1536]{1,0:T(8,128)(2,1)S(1)} %collective-permute-done.8.refs_0_), channel_id=1, source_target_pairs={{0,2},{1,3},{2,0},{3,1},{4,6},{5,7},{6,4},{7,5},{8,10},{9,11},{10,... | collective-permute-start | bytes 368648 | tf_op jit(solution)/shard_map/ppermute | solution.py:417
  50.2 3.1 %collective-permute-done.10.refs_2_ = bf16[40,1536]{1,0:T(8,128)(2,1)S(1)} collective-permute-done((bf16[40,1536]{1,0:T(8,128)(2,1)S(1)}, bf16[40,1536]{1,0:T(8,128)(2,1)S(1)}, u32[]{:S(2)}, u32[]{:S(2)}) %collective-permute-start.10) | collective-permute-done | bytes 122912 | tf_op jit(solution)/shard_map/ppermute | solution.py:417
  53.4 0.1 collective-permute-start.11
  53.4 0.2 own_half.6
  53.7 1.6 %collective-permute-done.11.other = bf16[160,1536]{1,0:T(8,128)(2,1)S(1)} collective-permute-done((bf16[160,1536]{1,0:T(8,128)(2,1)S(1)}, bf16[160,1536]{1,0:T(8,128)(2,1)S(1)}, u32[]{:S(2)}, u32[]{:S(2)}) %collective-permute-start.11) | collective-permute-done | bytes 491552 | tf_op jit(solution)/shard_map/ppermute | solution.py:417
  55.3 2.5 %collective-permute-start.12 = (bf16[40,1536]{1,0:T(8,128)(2,1)S(1)}, bf16[40,1536]{1,0:T(8,128)(2,1)S(1)}, u32[]{:S(2)}, u32[]{:S(2)}) collective-permute-start(bf16[40,1536]{1,0:T(8,128)(2,1)S(1)} %get-tuple-element.49), channel_id=1, source_target_pairs={{0,8},{1,9},{2,10},{3,11},{4,12},{5,13},{6,14},{7,15},{8,16},{9,17... | collective-permute-start | bytes 368648 | tf_op jit(solution)/shard_map/ppermute | solution.py:417
  57.8 0.7 collective-permute-start.13
  58.5 3.1 %collective-permute-done.12.refs_0_ = bf16[40,1536]{1,0:T(8,128)(2,1)S(1)} collective-permute-done((bf16[40,1536]{1,0:T(8,128)(2,1)S(1)}, bf16[40,1536]{1,0:T(8,128)(2,1)S(1)}, u32[]{:S(2)}, u32[]{:S(2)}) %collective-permute-start.12) | collective-permute-done | bytes 122912 | tf_op jit(solution)/shard_map/ppermute | solution.py:417
  61.6 1.7 %collective-permute-start.14 = (bf16[40,1536]{1,0:T(8,128)(2,1)S(1)}, bf16[40,1536]{1,0:T(8,128)(2,1)S(1)}, u32[]{:S(2)}, u32[]{:S(2)}) collective-permute-start(bf16[40,1536]{1,0:T(8,128)(2,1)S(1)} %collective-permute-done.12.refs_0_), channel_id=1, source_target_pairs={{0,2},{1,3},{2,0},{3,1},{4,6},{5,7},{6,4},{7,5},{8,10},{9,11},{10,... | collective-permute-start | bytes 368648 | tf_op jit(solution)/shard_map/ppermute | solution.py:417
  63.3 3.1 %collective-permute-done.14.refs_2_ = bf16[40,1536]{1,0:T(8,128)(2,1)S(1)} collective-permute-done((bf16[40,1536]{1,0:T(8,128)(2,1)S(1)}, bf16[40,1536]{1,0:T(8,128)(2,1)S(1)}, u32[]{:S(2)}, u32[]{:S(2)}) %collective-permute-start.14) | collective-permute-done | bytes 122912 | tf_op jit(solution)/shard_map/ppermute | solution.py:417
  66.5 0.1 collective-permute-start.15
  66.6 1.8 %collective-permute-done.15.other = bf16[160,1536]{1,0:T(8,128)(2,1)S(1)} collective-permute-done((bf16[160,1536]{1,0:T(8,128)(2,1)S(1)}, bf16[160,1536]{1,0:T(8,128)(2,1)S(1)}, u32[]{:S(2)}, u32[]{:S(2)}) %collective-permute-start.15) | collective-permute-done | bytes 491552 | tf_op jit(solution)/shard_map/ppermute | solution.py:417
  68.4 0.7 collective-permute-start.16
  69.1 0.7 collective-permute-start.17
  69.8 0.7 collective-permute-start.18
  70.5 1.3 %collective-permute-start.19 = (bf16[80,384]{1,0:T(8,128)(2,1)S(1)}, bf16[80,384]{1,0:T(8,128)(2,1)S(1)}, u32[]{:S(2)}, u32[]{:S(2)}) collective-permute-start(bf16[80,384]{1,0:T(8,128)(2,1)S(1)} %get-tuple-element.56), channel_id=1, source_target_pairs={{24,0},{25,4},{26,2},{27,6},{28,1},{29,5},{30,3},{31,7}} | collective-permute-start | bytes 184328 | tf_op jit(solution)/shard_map/ppermute | solution.py:417
  71.8 19.7 %collective-permute-done.19 = bf16[80,384]{1,0:T(8,128)(2,1)S(1)} collective-permute-done((bf16[80,384]{1,0:T(8,128)(2,1)S(1)}, bf16[80,384]{1,0:T(8,128)(2,1)S(1)}, u32[]{:S(2)}, u32[]{:S(2)}) %collective-permute-start.19) | collective-permute-done | bytes 61472 | tf_op jit(solution)/shard_map/ppermute | solution.py:417
  91.6 4.3 %collective-permute-start.20 = (bf16[40,384]{1,0:T(8,128)(2,1)S(1)}, bf16[40,384]{1,0:T(8,128)(2,1)S(1)}, u32[]{:S(2)}, u32[]{:S(2)}) collective-permute-start(bf16[40,384]{1,0:T(8,128)(2,1)S(1)} %get-tuple-element.62), channel_id=1, source_target_pairs={{0,1},{1,0},{2,3},{3,2},{4,5},{5,4},{6,7},{7,6},{8,9},{9,8},{10,11... | collective-permute-start | bytes 92168 | tf_op jit(solution)/shard_map/ppermute | solution.py:417
  95.9 0.9 collective-permute-done.20
  96.8 0.6 maximum_select_fusion
  (24 shorter events, 0.3 us)
Async XLA Ops:
  1.0 12.6 %collective-permute-start = (bf16[40,1536]{1,0:T(8,128)(2,1)S(1)}, bf16[40,1536]{1,0:T(8,128)(2,1)S(1)}, u32[]{:S(2)}, u32[]{:S(2)}) collective-permute-start(bf16[40,1536]{1,0:T(8,128)(2,1)S(1)} %get-tuple-element.60.refs_0_), channel_id=1, source_target_pairs={{16,2},{17,3},{18,0},{19,1},{20,6},{21,7},{22,4},{23,5}} | collective-permute-start | bytes 368648 | tf_op jit(solution)/shard_map/ppermute | solution.py:417
  2.3 12.9 %collective-permute-start.1 = (bf16[40,1536]{1,0:T(8,128)(2,1)S(1)}, bf16[40,1536]{1,0:T(8,128)(2,1)S(1)}, u32[]{:S(2)}, u32[]{:S(2)}) collective-permute-start(bf16[40,1536]{1,0:T(8,128)(2,1)S(1)} %get-tuple-element.59), channel_id=1, source_target_pairs={{24,4},{25,5},{26,6},{27,7},{28,0},{29,1},{30,2},{31,3}} | collective-permute-start | bytes 368648 | tf_op jit(solution)/shard_map/ppermute | solution.py:417
  3.6 11.6 %collective-permute-start.2 = (bf16[40,1536]{1,0:T(8,128)(2,1)S(1)}, bf16[40,1536]{1,0:T(8,128)(2,1)S(1)}, u32[]{:S(2)}, u32[]{:S(2)}) collective-permute-start(bf16[40,1536]{1,0:T(8,128)(2,1)S(1)} %get-tuple-element.59), channel_id=1, source_target_pairs={{8,6},{9,7},{10,4},{11,5},{12,2},{13,3},{14,0},{15,1}} | collective-permute-start | bytes 368648 | tf_op jit(solution)/shard_map/ppermute | solution.py:417
  4.9 10.4 %slice-start = ((s8[4718592]{0:T(1024)(128)(4,1)}), s8[4194304]{0:T(1024)(128)(4,1)S(1)}, s32[]{:S(2)}) async-start(s8[4718592]{0:T(1024)(128)(4,1)} %bitcast.9), calls=%async_computation | async-start | bytes 8388608
  5.7 0.9 copy-start
  6.6 0.7 copy-start.1
  7.2 0.7 copy-start.2
  7.9 7.5 %slice-start.1 = ((s8[4718592]{0:T(1024)(128)(4,1)}), s8[524288]{0:T(1024)(128)(4,1)S(1)}, s32[]{:S(2)}) async-start(s8[4718592]{0:T(1024)(128)(4,1)} %bitcast.9), calls=%async_computation.1 | async-start | bytes 1048576
  15.2 2.2 %collective-permute-start.3 = (bf16[160,1536]{1,0:T(8,128)(2,1)S(1)}, bf16[160,1536]{1,0:T(8,128)(2,1)S(1)}, u32[]{:S(2)}, u32[]{:S(2)}) collective-permute-start(bf16[160,1536]{1,0:T(8,128)(2,1)S(1)} %join_pieces.4.own), channel_id=1, source_target_pairs={{0,1},{1,0},{2,3},{3,2},{4,5},{5,4},{6,7},{7,6},{8,9},{9,8},{10,11... | collective-permute-start | bytes 1474568 | tf_op jit(solution)/shard_map/ppermute | solution.py:417
  28.2 6.6 %collective-permute-start.4 = (bf16[40,1536]{1,0:T(8,128)(2,1)S(1)}, bf16[40,1536]{1,0:T(8,128)(2,1)S(1)}, u32[]{:S(2)}, u32[]{:S(2)}) collective-permute-start(bf16[40,1536]{1,0:T(8,128)(2,1)S(1)} %get-tuple-element.39), channel_id=1, source_target_pairs={{0,8},{1,9},{2,10},{3,11},{4,12},{5,13},{6,14},{7,15},{8,16},{9,17... | collective-permute-start | bytes 368648 | tf_op jit(solution)/shard_map/ppermute | solution.py:417
  28.3 11.6 %collective-permute-start.5 = (bf16[80,1536]{1,0:T(8,128)(2,1)S(1)}, bf16[80,1536]{1,0:T(8,128)(2,1)S(1)}, u32[]{:S(2)}, u32[]{:S(2)}) collective-permute-start(bf16[80,1536]{1,0:T(8,128)(2,1)S(1)} %get-tuple-element.40), channel_id=1, source_target_pairs={{0,8},{1,9},{2,10},{3,11},{4,12},{5,13},{6,14},{7,15}} | collective-permute-start | bytes 737288 | tf_op jit(solution)/shard_map/ppermute | solution.py:417
  34.8 5.0 %collective-permute-start.6 = (bf16[40,1536]{1,0:T(8,128)(2,1)S(1)}, bf16[40,1536]{1,0:T(8,128)(2,1)S(1)}, u32[]{:S(2)}, u32[]{:S(2)}) collective-permute-start(bf16[40,1536]{1,0:T(8,128)(2,1)S(1)} %collective-permute-done.4.refs_0_), channel_id=1, source_target_pairs={{0,2},{1,3},{2,0},{3,1},{4,6},{5,7},{6,4},{7,5},{8,10},{9,11},{10,... | collective-permute-start | bytes 368648 | tf_op jit(solution)/shard_map/ppermute | solution.py:417
  39.9 1.9 %collective-permute-start.7 = (bf16[160,1536]{1,0:T(8,128)(2,1)S(1)}, bf16[160,1536]{1,0:T(8,128)(2,1)S(1)}, u32[]{:S(2)}, u32[]{:S(2)}) collective-permute-start(bf16[160,1536]{1,0:T(8,128)(2,1)S(1)} %join_pieces.5.own), channel_id=1, source_target_pairs={{0,1},{1,0},{2,3},{3,2},{4,5},{5,4},{6,7},{7,6},{8,9},{9,8},{10,11... | collective-permute-start | bytes 1474568 | tf_op jit(solution)/shard_map/ppermute | solution.py:417
  41.8 6.5 %collective-permute-start.8 = (bf16[40,1536]{1,0:T(8,128)(2,1)S(1)}, bf16[40,1536]{1,0:T(8,128)(2,1)S(1)}, u32[]{:S(2)}, u32[]{:S(2)}) collective-permute-start(bf16[40,1536]{1,0:T(8,128)(2,1)S(1)} %get-tuple-element.44), channel_id=1, source_target_pairs={{0,8},{1,9},{2,10},{3,11},{4,12},{5,13},{6,14},{7,15},{8,16},{9,17... | collective-permute-start | bytes 368648 | tf_op jit(solution)/shard_map/ppermute | solution.py:417
  45.1 8.2 %collective-permute-start.9 = (bf16[80,1536]{1,0:T(8,128)(2,1)S(1)}, bf16[80,1536]{1,0:T(8,128)(2,1)S(1)}, u32[]{:S(2)}, u32[]{:S(2)}) collective-permute-start(bf16[80,1536]{1,0:T(8,128)(2,1)S(1)} %get-tuple-element.45), channel_id=1, source_target_pairs={{8,16},{9,17},{10,18},{11,19},{12,20},{13,21},{14,22},{15,23}} | collective-permute-start | bytes 737288 | tf_op jit(solution)/shard_map/ppermute | solution.py:417
  48.3 5.0 %collective-permute-start.10 = (bf16[40,1536]{1,0:T(8,128)(2,1)S(1)}, bf16[40,1536]{1,0:T(8,128)(2,1)S(1)}, u32[]{:S(2)}, u32[]{:S(2)}) collective-permute-start(bf16[40,1536]{1,0:T(8,128)(2,1)S(1)} %collective-permute-done.8.refs_0_), channel_id=1, source_target_pairs={{0,2},{1,3},{2,0},{3,1},{4,6},{5,7},{6,4},{7,5},{8,10},{9,11},{10,... | collective-permute-start | bytes 368648 | tf_op jit(solution)/shard_map/ppermute | solution.py:417
  53.4 1.9 %collective-permute-start.11 = (bf16[160,1536]{1,0:T(8,128)(2,1)S(1)}, bf16[160,1536]{1,0:T(8,128)(2,1)S(1)}, u32[]{:S(2)}, u32[]{:S(2)}) collective-permute-start(bf16[160,1536]{1,0:T(8,128)(2,1)S(1)} %join_pieces.6.own), channel_id=1, source_target_pairs={{0,1},{1,0},{2,3},{3,2},{4,5},{5,4},{6,7},{7,6},{8,9},{9,8},{10,11... | collective-permute-start | bytes 1474568 | tf_op jit(solution)/shard_map/ppermute | solution.py:417
  55.3 6.3 %collective-permute-start.12 = (bf16[40,1536]{1,0:T(8,128)(2,1)S(1)}, bf16[40,1536]{1,0:T(8,128)(2,1)S(1)}, u32[]{:S(2)}, u32[]{:S(2)}) collective-permute-start(bf16[40,1536]{1,0:T(8,128)(2,1)S(1)} %get-tuple-element.49), channel_id=1, source_target_pairs={{0,8},{1,9},{2,10},{3,11},{4,12},{5,13},{6,14},{7,15},{8,16},{9,17... | collective-permute-start | bytes 368648 | tf_op jit(solution)/shard_map/ppermute | solution.py:417
  57.8 8.7 %collective-permute-start.13 = (bf16[80,1536]{1,0:T(8,128)(2,1)S(1)}, bf16[80,1536]{1,0:T(8,128)(2,1)S(1)}, u32[]{:S(2)}, u32[]{:S(2)}) collective-permute-start(bf16[80,1536]{1,0:T(8,128)(2,1)S(1)} %get-tuple-element.50), channel_id=1, source_target_pairs={{16,24},{17,25},{18,26},{19,27},{20,28},{21,29},{22,30},{23,31}} | collective-permute-start | bytes 737288 | tf_op jit(solution)/shard_map/ppermute | solution.py:417
  61.6 4.9 %collective-permute-start.14 = (bf16[40,1536]{1,0:T(8,128)(2,1)S(1)}, bf16[40,1536]{1,0:T(8,128)(2,1)S(1)}, u32[]{:S(2)}, u32[]{:S(2)}) collective-permute-start(bf16[40,1536]{1,0:T(8,128)(2,1)S(1)} %collective-permute-done.12.refs_0_), channel_id=1, source_target_pairs={{0,2},{1,3},{2,0},{3,1},{4,6},{5,7},{6,4},{7,5},{8,10},{9,11},{10,... | collective-permute-start | bytes 368648 | tf_op jit(solution)/shard_map/ppermute | solution.py:417
  66.5 1.9 %collective-permute-start.15 = (bf16[160,1536]{1,0:T(8,128)(2,1)S(1)}, bf16[160,1536]{1,0:T(8,128)(2,1)S(1)}, u32[]{:S(2)}, u32[]{:S(2)}) collective-permute-start(bf16[160,1536]{1,0:T(8,128)(2,1)S(1)} %join_pieces.7.own), channel_id=1, source_target_pairs={{0,1},{1,0},{2,3},{3,2},{4,5},{5,4},{6,7},{7,6},{8,9},{9,8},{10,11... | collective-permute-start | bytes 1474568 | tf_op jit(solution)/shard_map/ppermute | solution.py:417
  68.4 3.3 %collective-permute-start.16 = (bf16[80,384]{1,0:T(8,128)(2,1)S(1)}, bf16[80,384]{1,0:T(8,128)(2,1)S(1)}, u32[]{:S(2)}, u32[]{:S(2)}) collective-permute-start(bf16[80,384]{1,0:T(8,128)(2,1)S(1)} %get-tuple-element.55), channel_id=1, source_target_pairs={{25,28},{27,30},{28,25},{30,27}} | collective-permute-start | bytes 184328 | tf_op jit(solution)/shard_map/ppermute | solution.py:417
  69.1 2.7 %collective-permute-start.17 = (bf16[80,384]{1,0:T(8,128)(2,1)S(1)}, bf16[80,384]{1,0:T(8,128)(2,1)S(1)}, u32[]{:S(2)}, u32[]{:S(2)}) collective-permute-start(bf16[80,384]{1,0:T(8,128)(2,1)S(1)} %get-tuple-element.58), channel_id=1, source_target_pairs={{24,16},{25,20},{26,18},{27,22},{28,17},{29,21},{30,19},{31,23}} | collective-permute-start | bytes 184328 | tf_op jit(solution)/shard_map/ppermute | solution.py:417
  69.8 2.0 %collective-permute-start.18 = (bf16[80,384]{1,0:T(8,128)(2,1)S(1)}, bf16[80,384]{1,0:T(8,128)(2,1)S(1)}, u32[]{:S(2)}, u32[]{:S(2)}) collective-permute-start(bf16[80,384]{1,0:T(8,128)(2,1)S(1)} %get-tuple-element.57), channel_id=1, source_target_pairs={{24,8},{25,12},{26,10},{27,14},{28,9},{29,13},{30,11},{31,15}} | collective-permute-start | bytes 184328 | tf_op jit(solution)/shard_map/ppermute | solution.py:417
  70.5 21.1 %collective-permute-start.19 = (bf16[80,384]{1,0:T(8,128)(2,1)S(1)}, bf16[80,384]{1,0:T(8,128)(2,1)S(1)}, u32[]{:S(2)}, u32[]{:S(2)}) collective-permute-start(bf16[80,384]{1,0:T(8,128)(2,1)S(1)} %get-tuple-element.56), channel_id=1, source_target_pairs={{24,0},{25,4},{26,2},{27,6},{28,1},{29,5},{30,3},{31,7}} | collective-permute-start | bytes 184328 | tf_op jit(solution)/shard_map/ppermute | solution.py:417
  91.6 5.2 %collective-permute-start.20 = (bf16[40,384]{1,0:T(8,128)(2,1)S(1)}, bf16[40,384]{1,0:T(8,128)(2,1)S(1)}, u32[]{:S(2)}, u32[]{:S(2)}) collective-permute-start(bf16[40,384]{1,0:T(8,128)(2,1)S(1)} %get-tuple-element.62), channel_id=1, source_target_pairs={{0,1},{1,0},{2,3},{3,2},{4,5},{5,4},{6,7},{7,6},{8,9},{9,8},{10,11... | collective-permute-start | bytes 92168 | tf_op jit(solution)/shard_map/ppermute | solution.py:417

commit v2 on v1

--- a/solution.py
+++ b/solution.py
@@ -461,7 +461,7 @@
     crossed = own[:, final * cols :]
     crossing = [s for s in seqs if crosses(s)]
     mine = None
-    for t in range(final):
+    for t in reversed(range(final)):
         here = sent(own[:, t * cols : (t + 1) * cols], seq_count, [((final, s), (t, target(s))) for s in seqs])
         mine = here if mine is None else jnp.where(section == t, here, mine)
     crossed = sent(crossed, seq_count, [((final, s), (final, target(s))) for s in crossing])

time: 97.7 us -> 89.4 us (0.915)
  Pallas kernels: 18.9 us -> 11.8 us
  waiting for transfers between devices: 47.9 us -> 45.6 us
    pallas_call x4, Pallas kernels: 10.7 us -> 3.65 us  [run_stage(): pl.pallas_call(functools.partial(stage_kernel, head_dim, micro_count, sta...]
    ppermute x21, waiting for transfers between devices: 47.9 us -> 45.6 us  [sent(): return lax.ppermute(value, ('section', 'seq'), flat)]
  transfers between devices with their start and end apart: 21 -> 21, of which waited for: 12 -> 12; matrix products, arithmetic and copies ran while one was open for 0% -> 0% of each run, Pallas kernels for 8% -> 9%
where the time goes in v2:
time: 89.4 us; the launch traced here: 88.9 us
  waiting for transfers between devices  45.6 us (51%)
  starting transfers between devices  26.6 us (30%)
  Pallas kernels  11.8 us (13%)
  local copies, waits for them, and re-layouts  3.18 us (4%)
  between operations  1.11 us (1%)
    ppermute x21, waiting for transfers between devices, sent(): return lax.ppermute(value, ('section', 'seq'), flat)  45.6 us
    ppermute x21, starting transfers between devices, sent(): return lax.ppermute(value, ('section', 'seq'), flat)  26.6 us
    pallas_call x1, Pallas kernels, keep_weights(): pl.pallas_call(functools.partial(keep_kernel, head_dim), out_shape=[pltpu...  5.69 us
    pallas_call x4, Pallas kernels, run_stage(): pl.pallas_call(functools.partial(stage_kernel, head_dim, micro_count, sta...  3.65 us
    unnamed x10, local copies, waits for them, and re-layouts  2.17 us
    pallas_call x4, Pallas kernels, run_stage(): pl.pallas_call(functools.partial(own_kernel, head_dim, stage), out_shape=...  2.01 us
  transfers between devices with their start and end apart: 21, of which 12 were waited for; matrix products, arithmetic and copies ran while one was open for 0% of the time, Pallas kernels for 9%

profile of v2, /device:TPU:0, one launch (start us, length us, event | category | flops | bytes accessed | tf_op | source)
XLA Modules:
  0.0 88.9 jit_solution(8808517922467921107)
XLA Ops:
  0.0 1.0 %dynamic-slice_bitcast_fusion = (bf16[40,1536]{1,0:T(8,128)(2,1)S(1)}, bf16[40,1536]{1,0:T(8,128)(2,1)S(1)}) fusion(bf16[2,40,1536]{2,1,0:T(8,128)(2,1)} %param.7, s32[]{:T(128)S(6)} %select_n.81, s32[]{:T(128)S(6)} %select_n.80), kind=kLoop, calls=%fused_computation | loop fusion | bytes 491528 | tf_op jit(solution)/shard_map/jit(dynamic_index_in_dim)/squeeze | solution.py:432
  1.0 1.3 %collective-permute-start = (bf16[40,1536]{1,0:T(8,128)(2,1)S(1)}, bf16[40,1536]{1,0:T(8,128)(2,1)S(1)}, u32[]{:S(2)}, u32[]{:S(2)}) collective-permute-start(bf16[40,1536]{1,0:T(8,128)(2,1)S(1)} %get-tuple-element.60.refs_0_), channel_id=1, source_target_pairs={{16,2},{17,3},{18,0},{19,1},{20,6},{21,7},{22,4},{23,5}} | collective-permute-start | bytes 368648 | tf_op jit(solution)/shard_map/ppermute | solution.py:417
  2.3 1.3 %collective-permute-start.1 = (bf16[40,1536]{1,0:T(8,128)(2,1)S(1)}, bf16[40,1536]{1,0:T(8,128)(2,1)S(1)}, u32[]{:S(2)}, u32[]{:S(2)}) collective-permute-start(bf16[40,1536]{1,0:T(8,128)(2,1)S(1)} %get-tuple-element.59), channel_id=1, source_target_pairs={{24,4},{25,5},{26,6},{27,7},{28,0},{29,1},{30,2},{31,3}} | collective-permute-start | bytes 368648 | tf_op jit(solution)/shard_map/ppermute | solution.py:417
  3.6 1.3 %collective-permute-start.2 = (bf16[40,1536]{1,0:T(8,128)(2,1)S(1)}, bf16[40,1536]{1,0:T(8,128)(2,1)S(1)}, u32[]{:S(2)}, u32[]{:S(2)}) collective-permute-start(bf16[40,1536]{1,0:T(8,128)(2,1)S(1)} %get-tuple-element.59), channel_id=1, source_target_pairs={{8,6},{9,7},{10,4},{11,5},{12,2},{13,3},{14,0},{15,1}} | collective-permute-start | bytes 368648 | tf_op jit(solution)/shard_map/ppermute | solution.py:417
  4.9 0.0 slice-start
  5.7 0.0 copy-start
  5.7 0.8 copy-done
  6.6 0.7 copy-done.1
  7.2 0.7 copy-done.2
  7.9 5.7 %keep_weights.1 = (bf16[2,1536,2304]{2,1,0:T(8,128)(2,1)S(1)}, f32[2,1536]{1,0:T(2,128)S(1)}, f32[4,256]{1,0:T(4,128)S(1)}, f32[4,1280]{1,0:T(4,128)S(1)}, bf16[...) custom-call(s32[2]{0:T(128)S(1)} %copy-done.1, s32[1]{0:T(128)S(6)} %copy.32.layers, bf16[2,1536,2304]{2,1,0:T(8,128)(2,1)} %qkv_hbm.1, ...), custom_call_target="tpu_custom_call" | custom-call | bytes 28311552 | tf_op jit(solution)/shard_map/keep_weights/pallas_call | solution.py:237
  13.6 0.0 collective-permute-done.refs_1_
  13.6 1.6 %collective-permute-done.1.refs_2_ = bf16[40,1536]{1,0:T(8,128)(2,1)S(1)} collective-permute-done((bf16[40,1536]{1,0:T(8,128)(2,1)S(1)}, bf16[40,1536]{1,0:T(8,128)(2,1)S(1)}, u32[]{:S(2)}, u32[]{:S(2)}) %collective-permute-start.1) | collective-permute-done | bytes 122912 | tf_op jit(solution)/shard_map/ppermute | solution.py:417
  15.2 0.0 collective-permute-done.2.refs_3_
  15.2 0.1 collective-permute-start.3
  15.3 0.3 keep_out.1.out_w
  15.7 1.8 %own_half.4 = (bf16[3,1280,256]{2,1,0:T(8,128)(2,1)S(1)}, bf16[3,1280,256]{2,1,0:T(8,128)(2,1)S(1)}, bf16[320,768]{1,0:T(8,128)(2,1)S(1)}) custom-call(bf16[160,1536]{1,0:T(8,128)(2,1)S(1)} %join_pieces.4.own, bf16[2,1536,2304]{2,1,0:T(8,128)(2,1)S(1)} %get-tuple-element.31.qkv_w, f32[2,1536]{1,0:T(2,128)S(1)} %get-tuple-element.32.norm_g, ...), custom_call_target="tpu_custom_call" | custom-call | flops 1132462080 | tf_op jit(solution)/shard_map/own_half/pallas_call | solution.py:386
  17.5 0.0 collective-permute-done.3.other
  17.5 3.6 %stage.4 = (bf16[40,1536]{1,0:T(8,128)(2,1)S(1)}, bf16[80,1536]{1,0:T(8,128)(2,1)S(1)}, bf16[3,1280,256]{2,1,0:T(8,128)(2,1)S(1)}, bf16[3,1280,256]{2,1,0:T(8,128)(2,1)S(1)}, bf16[320,768]{1,0:T(8,128)(2,1)S(1)}) custom-call(s32[1]{0:T(128)S(6)} %copy.32.layers, ...), custom_call_target="tpu_custom_call", output_to_operand_aliasing={{2}: (9, {}), {3}: (10, {}), {4}: (11, {})} | custom-call | tf_op jit(solution)/shard_map/stage/pallas_call | solution.py:398
  21.1 1.6 %collective-permute-start.4 = (bf16[40,1536]{1,0:T(8,128)(2,1)S(1)}, bf16[40,1536]{1,0:T(8,128)(2,1)S(1)}, u32[]{:S(2)}, u32[]{:S(2)}) collective-permute-start(bf16[40,1536]{1,0:T(8,128)(2,1)S(1)} %get-tuple-element.39), channel_id=1, source_target_pairs={{0,8},{1,9},{2,10},{3,11},{4,12},{5,13},{6,14},{7,15},{8,16},{9,17... | collective-permute-start | bytes 368648 | tf_op jit(solution)/shard_map/ppermute | solution.py:417
  22.7 1.9 %collective-permute-start.5 = (bf16[80,1536]{1,0:T(8,128)(2,1)S(1)}, bf16[80,1536]{1,0:T(8,128)(2,1)S(1)}, u32[]{:S(2)}, u32[]{:S(2)}) collective-permute-start(bf16[80,1536]{1,0:T(8,128)(2,1)S(1)} %get-tuple-element.40), channel_id=1, source_target_pairs={{0,8},{1,9},{2,10},{3,11},{4,12},{5,13},{6,14},{7,15}} | collective-permute-start | bytes 737288 | tf_op jit(solution)/shard_map/ppermute | solution.py:417
  24.6 3.1 %collective-permute-done.4.refs_0_ = bf16[40,1536]{1,0:T(8,128)(2,1)S(1)} collective-permute-done((bf16[40,1536]{1,0:T(8,128)(2,1)S(1)}, bf16[40,1536]{1,0:T(8,128)(2,1)S(1)}, u32[]{:S(2)}, u32[]{:S(2)}) %collective-permute-start.4) | collective-permute-done | bytes 122912 | tf_op jit(solution)/shard_map/ppermute | solution.py:417
  27.8 1.9 %collective-permute-start.6 = (bf16[40,1536]{1,0:T(8,128)(2,1)S(1)}, bf16[40,1536]{1,0:T(8,128)(2,1)S(1)}, u32[]{:S(2)}, u32[]{:S(2)}) collective-permute-start(bf16[40,1536]{1,0:T(8,128)(2,1)S(1)} %collective-permute-done.4.refs_0_), channel_id=1, source_target_pairs={{0,2},{1,3},{2,0},{3,1},{4,6},{5,7},{6,4},{7,5},{8,10},{9,11},{10,... | collective-permute-start | bytes 368648 | tf_op jit(solution)/shard_map/ppermute | solution.py:417
  29.6 3.2 %collective-permute-done.6.refs_2_ = bf16[40,1536]{1,0:T(8,128)(2,1)S(1)} collective-permute-done((bf16[40,1536]{1,0:T(8,128)(2,1)S(1)}, bf16[40,1536]{1,0:T(8,128)(2,1)S(1)}, u32[]{:S(2)}, u32[]{:S(2)}) %collective-permute-start.6) | collective-permute-done | bytes 122912 | tf_op jit(solution)/shard_map/ppermute | solution.py:417
  32.8 0.1 collective-permute-start.7
  32.9 1.8 %collective-permute-done.7.other = bf16[160,1536]{1,0:T(8,128)(2,1)S(1)} collective-permute-done((bf16[160,1536]{1,0:T(8,128)(2,1)S(1)}, bf16[160,1536]{1,0:T(8,128)(2,1)S(1)}, u32[]{:S(2)}, u32[]{:S(2)}) %collective-permute-start.7) | collective-permute-done | bytes 491552 | tf_op jit(solution)/shard_map/ppermute | solution.py:417
  34.8 4.6 %collective-permute-start.8 = (bf16[40,1536]{1,0:T(8,128)(2,1)S(1)}, bf16[40,1536]{1,0:T(8,128)(2,1)S(1)}, u32[]{:S(2)}, u32[]{:S(2)}) collective-permute-start(bf16[40,1536]{1,0:T(8,128)(2,1)S(1)} %get-tuple-element.44), channel_id=1, source_target_pairs={{0,8},{1,9},{2,10},{3,11},{4,12},{5,13},{6,14},{7,15},{8,16},{9,17... | collective-permute-start | bytes 368648 | tf_op jit(solution)/shard_map/ppermute | solution.py:417
  39.3 0.7 collective-permute-start.9
  40.0 2.5 %collective-permute-done.8.refs_0_ = bf16[40,1536]{1,0:T(8,128)(2,1)S(1)} collective-permute-done((bf16[40,1536]{1,0:T(8,128)(2,1)S(1)}, bf16[40,1536]{1,0:T(8,128)(2,1)S(1)}, u32[]{:S(2)}, u32[]{:S(2)}) %collective-permute-start.8) | collective-permute-done | bytes 122912 | tf_op jit(solution)/shard_map/ppermute | solution.py:417
  42.5 0.6 collective-permute-start.10
  43.1 4.3 %collective-permute-done.10.refs_2_ = bf16[40,1536]{1,0:T(8,128)(2,1)S(1)} collective-permute-done((bf16[40,1536]{1,0:T(8,128)(2,1)S(1)}, bf16[40,1536]{1,0:T(8,128)(2,1)S(1)}, u32[]{:S(2)}, u32[]{:S(2)}) %collective-permute-start.10) | collective-permute-done | bytes 122912 | tf_op jit(solution)/shard_map/ppermute | solution.py:417
  47.5 0.1 collective-permute-start.11
  47.5 0.2 own_half.6
  47.7 1.6 %collective-permute-done.11.other = bf16[160,1536]{1,0:T(8,128)(2,1)S(1)} collective-permute-done((bf16[160,1536]{1,0:T(8,128)(2,1)S(1)}, bf16[160,1536]{1,0:T(8,128)(2,1)S(1)}, u32[]{:S(2)}, u32[]{:S(2)}) %collective-permute-start.11) | collective-permute-done | bytes 491552 | tf_op jit(solution)/shard_map/ppermute | solution.py:417
  49.4 2.5 %collective-permute-start.12 = (bf16[40,1536]{1,0:T(8,128)(2,1)S(1)}, bf16[40,1536]{1,0:T(8,128)(2,1)S(1)}, u32[]{:S(2)}, u32[]{:S(2)}) collective-permute-start(bf16[40,1536]{1,0:T(8,128)(2,1)S(1)} %get-tuple-element.49), channel_id=1, source_target_pairs={{0,8},{1,9},{2,10},{3,11},{4,12},{5,13},{6,14},{7,15},{8,16},{9,17... | collective-permute-start | bytes 368648 | tf_op jit(solution)/shard_map/ppermute | solution.py:417
  51.9 0.7 collective-permute-start.13
  52.5 3.1 %collective-permute-done.12.refs_0_ = bf16[40,1536]{1,0:T(8,128)(2,1)S(1)} collective-permute-done((bf16[40,1536]{1,0:T(8,128)(2,1)S(1)}, bf16[40,1536]{1,0:T(8,128)(2,1)S(1)}, u32[]{:S(2)}, u32[]{:S(2)}) %collective-permute-start.12) | collective-permute-done | bytes 122912 | tf_op jit(solution)/shard_map/ppermute | solution.py:417
  55.6 0.6 collective-permute-start.14
  56.2 4.3 %collective-permute-done.14.refs_2_ = bf16[40,1536]{1,0:T(8,128)(2,1)S(1)} collective-permute-done((bf16[40,1536]{1,0:T(8,128)(2,1)S(1)}, bf16[40,1536]{1,0:T(8,128)(2,1)S(1)}, u32[]{:S(2)}, u32[]{:S(2)}) %collective-permute-start.14) | collective-permute-done | bytes 122912 | tf_op jit(solution)/shard_map/ppermute | solution.py:417
  60.6 0.1 collective-permute-start.15
  60.7 1.8 %collective-permute-done.15.other = bf16[160,1536]{1,0:T(8,128)(2,1)S(1)} collective-permute-done((bf16[160,1536]{1,0:T(8,128)(2,1)S(1)}, bf16[160,1536]{1,0:T(8,128)(2,1)S(1)}, u32[]{:S(2)}, u32[]{:S(2)}) %collective-permute-start.15) | collective-permute-done | bytes 491552 | tf_op jit(solution)/shard_map/ppermute | solution.py:417
  62.5 0.7 collective-permute-start.16
  63.2 1.3 %collective-permute-start.17 = (bf16[80,384]{1,0:T(8,128)(2,1)S(1)}, bf16[80,384]{1,0:T(8,128)(2,1)S(1)}, u32[]{:S(2)}, u32[]{:S(2)}) collective-permute-start(bf16[80,384]{1,0:T(8,128)(2,1)S(1)} %get-tuple-element.58), channel_id=1, source_target_pairs={{24,0},{25,4},{26,2},{27,6},{28,1},{29,5},{30,3},{31,7}} | collective-permute-start | bytes 184328 | tf_op jit(solution)/shard_map/ppermute | solution.py:417
  64.5 0.7 collective-permute-start.18
  65.2 0.7 collective-permute-start.19
  65.9 17.3 %collective-permute-done.17 = bf16[80,384]{1,0:T(8,128)(2,1)S(1)} collective-permute-done((bf16[80,384]{1,0:T(8,128)(2,1)S(1)}, bf16[80,384]{1,0:T(8,128)(2,1)S(1)}, u32[]{:S(2)}, u32[]{:S(2)}) %collective-permute-start.17) | collective-permute-done | bytes 61472 | tf_op jit(solution)/shard_map/ppermute | solution.py:417
  83.2 4.2 %collective-permute-start.20 = (bf16[40,384]{1,0:T(8,128)(2,1)S(1)}, bf16[40,384]{1,0:T(8,128)(2,1)S(1)}, u32[]{:S(2)}, u32[]{:S(2)}) collective-permute-start(bf16[40,384]{1,0:T(8,128)(2,1)S(1)} %get-tuple-element.62), channel_id=1, source_target_pairs={{0,1},{1,0},{2,3},{3,2},{4,5},{5,4},{6,7},{7,6},{8,9},{9,8},{10,11... | collective-permute-start | bytes 92168 | tf_op jit(solution)/shard_map/ppermute | solution.py:417
  87.4 0.9 collective-permute-done.20
  88.3 0.6 maximum_select_fusion
  (24 shorter events, 0.3 us)
Async XLA Ops:
  1.0 12.6 %collective-permute-start = (bf16[40,1536]{1,0:T(8,128)(2,1)S(1)}, bf16[40,1536]{1,0:T(8,128)(2,1)S(1)}, u32[]{:S(2)}, u32[]{:S(2)}) collective-permute-start(bf16[40,1536]{1,0:T(8,128)(2,1)S(1)} %get-tuple-element.60.refs_0_), channel_id=1, source_target_pairs={{16,2},{17,3},{18,0},{19,1},{20,6},{21,7},{22,4},{23,5}} | collective-permute-start | bytes 368648 | tf_op jit(solution)/shard_map/ppermute | solution.py:417
  2.3 12.9 %collective-permute-start.1 = (bf16[40,1536]{1,0:T(8,128)(2,1)S(1)}, bf16[40,1536]{1,0:T(8,128)(2,1)S(1)}, u32[]{:S(2)}, u32[]{:S(2)}) collective-permute-start(bf16[40,1536]{1,0:T(8,128)(2,1)S(1)} %get-tuple-element.59), channel_id=1, source_target_pairs={{24,4},{25,5},{26,6},{27,7},{28,0},{29,1},{30,2},{31,3}} | collective-permute-start | bytes 368648 | tf_op jit(solution)/shard_map/ppermute | solution.py:417
  3.6 11.6 %collective-permute-start.2 = (bf16[40,1536]{1,0:T(8,128)(2,1)S(1)}, bf16[40,1536]{1,0:T(8,128)(2,1)S(1)}, u32[]{:S(2)}, u32[]{:S(2)}) collective-permute-start(bf16[40,1536]{1,0:T(8,128)(2,1)S(1)} %get-tuple-element.59), channel_id=1, source_target_pairs={{8,6},{9,7},{10,4},{11,5},{12,2},{13,3},{14,0},{15,1}} | collective-permute-start | bytes 368648 | tf_op jit(solution)/shard_map/ppermute | solution.py:417
  4.9 10.4 %slice-start = ((s8[4718592]{0:T(1024)(128)(4,1)}), s8[4194304]{0:T(1024)(128)(4,1)S(1)}, s32[]{:S(2)}) async-start(s8[4718592]{0:T(1024)(128)(4,1)} %bitcast.9), calls=%async_computation | async-start | bytes 8388608
  5.7 0.9 copy-start
  6.6 0.7 copy-start.1
  7.2 0.7 copy-start.2
  7.9 7.5 %slice-start.1 = ((s8[4718592]{0:T(1024)(128)(4,1)}), s8[524288]{0:T(1024)(128)(4,1)S(1)}, s32[]{:S(2)}) async-start(s8[4718592]{0:T(1024)(128)(4,1)} %bitcast.9), calls=%async_computation.1 | async-start | bytes 1048576
  15.2 2.2 %collective-permute-start.3 = (bf16[160,1536]{1,0:T(8,128)(2,1)S(1)}, bf16[160,1536]{1,0:T(8,128)(2,1)S(1)}, u32[]{:S(2)}, u32[]{:S(2)}) collective-permute-start(bf16[160,1536]{1,0:T(8,128)(2,1)S(1)} %join_pieces.4.own), channel_id=1, source_target_pairs={{0,1},{1,0},{2,3},{3,2},{4,5},{5,4},{6,7},{7,6},{8,9},{9,8},{10,11... | collective-permute-start | bytes 1474568 | tf_op jit(solution)/shard_map/ppermute | solution.py:417
  21.1 6.6 %collective-permute-start.4 = (bf16[40,1536]{1,0:T(8,128)(2,1)S(1)}, bf16[40,1536]{1,0:T(8,128)(2,1)S(1)}, u32[]{:S(2)}, u32[]{:S(2)}) collective-permute-start(bf16[40,1536]{1,0:T(8,128)(2,1)S(1)} %get-tuple-element.39), channel_id=1, source_target_pairs={{0,8},{1,9},{2,10},{3,11},{4,12},{5,13},{6,14},{7,15},{8,16},{9,17... | collective-permute-start | bytes 368648 | tf_op jit(solution)/shard_map/ppermute | solution.py:417
  22.7 10.1 %collective-permute-start.5 = (bf16[80,1536]{1,0:T(8,128)(2,1)S(1)}, bf16[80,1536]{1,0:T(8,128)(2,1)S(1)}, u32[]{:S(2)}, u32[]{:S(2)}) collective-permute-start(bf16[80,1536]{1,0:T(8,128)(2,1)S(1)} %get-tuple-element.40), channel_id=1, source_target_pairs={{0,8},{1,9},{2,10},{3,11},{4,12},{5,13},{6,14},{7,15}} | collective-permute-start | bytes 737288 | tf_op jit(solution)/shard_map/ppermute | solution.py:417
  27.8 5.0 %collective-permute-start.6 = (bf16[40,1536]{1,0:T(8,128)(2,1)S(1)}, bf16[40,1536]{1,0:T(8,128)(2,1)S(1)}, u32[]{:S(2)}, u32[]{:S(2)}) collective-permute-start(bf16[40,1536]{1,0:T(8,128)(2,1)S(1)} %collective-permute-done.4.refs_0_), channel_id=1, source_target_pairs={{0,2},{1,3},{2,0},{3,1},{4,6},{5,7},{6,4},{7,5},{8,10},{9,11},{10,... | collective-permute-start | bytes 368648 | tf_op jit(solution)/shard_map/ppermute | solution.py:417
  32.8 1.9 %collective-permute-start.7 = (bf16[160,1536]{1,0:T(8,128)(2,1)S(1)}, bf16[160,1536]{1,0:T(8,128)(2,1)S(1)}, u32[]{:S(2)}, u32[]{:S(2)}) collective-permute-start(bf16[160,1536]{1,0:T(8,128)(2,1)S(1)} %join_pieces.5.own), channel_id=1, source_target_pairs={{0,1},{1,0},{2,3},{3,2},{4,5},{5,4},{6,7},{7,6},{8,9},{9,8},{10,11... | collective-permute-start | bytes 1474568 | tf_op jit(solution)/shard_map/ppermute | solution.py:417
  34.8 7.8 %collective-permute-start.8 = (bf16[40,1536]{1,0:T(8,128)(2,1)S(1)}, bf16[40,1536]{1,0:T(8,128)(2,1)S(1)}, u32[]{:S(2)}, u32[]{:S(2)}) collective-permute-start(bf16[40,1536]{1,0:T(8,128)(2,1)S(1)} %get-tuple-element.44), channel_id=1, source_target_pairs={{0,8},{1,9},{2,10},{3,11},{4,12},{5,13},{6,14},{7,15},{8,16},{9,17... | collective-permute-start | bytes 368648 | tf_op jit(solution)/shard_map/ppermute | solution.py:417
  39.3 8.1 %collective-permute-start.9 = (bf16[80,1536]{1,0:T(8,128)(2,1)S(1)}, bf16[80,1536]{1,0:T(8,128)(2,1)S(1)}, u32[]{:S(2)}, u32[]{:S(2)}) collective-permute-start(bf16[80,1536]{1,0:T(8,128)(2,1)S(1)} %get-tuple-element.45), channel_id=1, source_target_pairs={{8,16},{9,17},{10,18},{11,19},{12,20},{13,21},{14,22},{15,23}} | collective-permute-start | bytes 737288 | tf_op jit(solution)/shard_map/ppermute | solution.py:417
  42.5 4.9 %collective-permute-start.10 = (bf16[40,1536]{1,0:T(8,128)(2,1)S(1)}, bf16[40,1536]{1,0:T(8,128)(2,1)S(1)}, u32[]{:S(2)}, u32[]{:S(2)}) collective-permute-start(bf16[40,1536]{1,0:T(8,128)(2,1)S(1)} %collective-permute-done.8.refs_0_), channel_id=1, source_target_pairs={{0,2},{1,3},{2,0},{3,1},{4,6},{5,7},{6,4},{7,5},{8,10},{9,11},{10,... | collective-permute-start | bytes 368648 | tf_op jit(solution)/shard_map/ppermute | solution.py:417
  47.5 1.9 %collective-permute-start.11 = (bf16[160,1536]{1,0:T(8,128)(2,1)S(1)}, bf16[160,1536]{1,0:T(8,128)(2,1)S(1)}, u32[]{:S(2)}, u32[]{:S(2)}) collective-permute-start(bf16[160,1536]{1,0:T(8,128)(2,1)S(1)} %join_pieces.6.own), channel_id=1, source_target_pairs={{0,1},{1,0},{2,3},{3,2},{4,5},{5,4},{6,7},{7,6},{8,9},{9,8},{10,11... | collective-permute-start | bytes 1474568 | tf_op jit(solution)/shard_map/ppermute | solution.py:417
  49.4 6.3 %collective-permute-start.12 = (bf16[40,1536]{1,0:T(8,128)(2,1)S(1)}, bf16[40,1536]{1,0:T(8,128)(2,1)S(1)}, u32[]{:S(2)}, u32[]{:S(2)}) collective-permute-start(bf16[40,1536]{1,0:T(8,128)(2,1)S(1)} %get-tuple-element.49), channel_id=1, source_target_pairs={{0,8},{1,9},{2,10},{3,11},{4,12},{5,13},{6,14},{7,15},{8,16},{9,17... | collective-permute-start | bytes 368648 | tf_op jit(solution)/shard_map/ppermute | solution.py:417
  51.9 8.7 %collective-permute-start.13 = (bf16[80,1536]{1,0:T(8,128)(2,1)S(1)}, bf16[80,1536]{1,0:T(8,128)(2,1)S(1)}, u32[]{:S(2)}, u32[]{:S(2)}) collective-permute-start(bf16[80,1536]{1,0:T(8,128)(2,1)S(1)} %get-tuple-element.50), channel_id=1, source_target_pairs={{16,24},{17,25},{18,26},{19,27},{20,28},{21,29},{22,30},{23,31}} | collective-permute-start | bytes 737288 | tf_op jit(solution)/shard_map/ppermute | solution.py:417
  55.6 4.9 %collective-permute-start.14 = (bf16[40,1536]{1,0:T(8,128)(2,1)S(1)}, bf16[40,1536]{1,0:T(8,128)(2,1)S(1)}, u32[]{:S(2)}, u32[]{:S(2)}) collective-permute-start(bf16[40,1536]{1,0:T(8,128)(2,1)S(1)} %collective-permute-done.12.refs_0_), channel_id=1, source_target_pairs={{0,2},{1,3},{2,0},{3,1},{4,6},{5,7},{6,4},{7,5},{8,10},{9,11},{10,... | collective-permute-start | bytes 368648 | tf_op jit(solution)/shard_map/ppermute | solution.py:417
  60.6 1.9 %collective-permute-start.15 = (bf16[160,1536]{1,0:T(8,128)(2,1)S(1)}, bf16[160,1536]{1,0:T(8,128)(2,1)S(1)}, u32[]{:S(2)}, u32[]{:S(2)}) collective-permute-start(bf16[160,1536]{1,0:T(8,128)(2,1)S(1)} %join_pieces.7.own), channel_id=1, source_target_pairs={{0,1},{1,0},{2,3},{3,2},{4,5},{5,4},{6,7},{7,6},{8,9},{9,8},{10,11... | collective-permute-start | bytes 1474568 | tf_op jit(solution)/shard_map/ppermute | solution.py:417
  62.5 3.3 %collective-permute-start.16 = (bf16[80,384]{1,0:T(8,128)(2,1)S(1)}, bf16[80,384]{1,0:T(8,128)(2,1)S(1)}, u32[]{:S(2)}, u32[]{:S(2)}) collective-permute-start(bf16[80,384]{1,0:T(8,128)(2,1)S(1)} %get-tuple-element.55), channel_id=1, source_target_pairs={{25,28},{27,30},{28,25},{30,27}} | collective-permute-start | bytes 184328 | tf_op jit(solution)/shard_map/ppermute | solution.py:417
  63.2 20.0 %collective-permute-start.17 = (bf16[80,384]{1,0:T(8,128)(2,1)S(1)}, bf16[80,384]{1,0:T(8,128)(2,1)S(1)}, u32[]{:S(2)}, u32[]{:S(2)}) collective-permute-start(bf16[80,384]{1,0:T(8,128)(2,1)S(1)} %get-tuple-element.58), channel_id=1, source_target_pairs={{24,0},{25,4},{26,2},{27,6},{28,1},{29,5},{30,3},{31,7}} | collective-permute-start | bytes 184328 | tf_op jit(solution)/shard_map/ppermute | solution.py:417
  64.5 18.7 %collective-permute-start.18 = (bf16[80,384]{1,0:T(8,128)(2,1)S(1)}, bf16[80,384]{1,0:T(8,128)(2,1)S(1)}, u32[]{:S(2)}, u32[]{:S(2)}) collective-permute-start(bf16[80,384]{1,0:T(8,128)(2,1)S(1)} %get-tuple-element.57), channel_id=1, source_target_pairs={{24,8},{25,12},{26,10},{27,14},{28,9},{29,13},{30,11},{31,15}} | collective-permute-start | bytes 184328 | tf_op jit(solution)/shard_map/ppermute | solution.py:417
  65.2 18.0 %collective-permute-start.19 = (bf16[80,384]{1,0:T(8,128)(2,1)S(1)}, bf16[80,384]{1,0:T(8,128)(2,1)S(1)}, u32[]{:S(2)}, u32[]{:S(2)}) collective-permute-start(bf16[80,384]{1,0:T(8,128)(2,1)S(1)} %get-tuple-element.56), channel_id=1, source_target_pairs={{24,16},{25,20},{26,18},{27,22},{28,17},{29,21},{30,19},{31,23}} | collective-permute-start | bytes 184328 | tf_op jit(solution)/shard_map/ppermute | solution.py:417
  83.2 5.1 %collective-permute-start.20 = (bf16[40,384]{1,0:T(8,128)(2,1)S(1)}, bf16[40,384]{1,0:T(8,128)(2,1)S(1)}, u32[]{:S(2)}, u32[]{:S(2)}) collective-permute-start(bf16[40,384]{1,0:T(8,128)(2,1)S(1)} %get-tuple-element.62), channel_id=1, source_target_pairs={{0,1},{1,0},{2,3},{3,2},{4,5},{5,4},{6,7},{7,6},{8,9},{9,8},{10,11... | collective-permute-start | bytes 92168 | tf_op jit(solution)/shard_map/ppermute | solution.py:417
